TPU v7x, 256 devices: a whole 4x4x8 slice. The times are simulated.
256 devices in a mesh: tm: 64 (over x_hi, y, z), chan: 4 (over x_lo, core).
Axes of the slice: x: 4 (x_hi: 2, x_lo: 2; x = x_hi * 2 + x_lo), y: 4, z: 8, core: 2. Of those that a mesh axis runs over, the one named last changes fastest.
Arguments:
- tokens: bfloat16 [131072, 1024], P('tm', 'chan'), may hold values from -170 to 170
- w_query: bfloat16 [1024, 1024], P(None, 'chan'), may hold values from -0.1875 to 0.1875
- w_key: bfloat16 [1024, 1024], P(None, 'chan'), may hold values from -0.1875 to 0.1875
- w_value: bfloat16 [1024, 1024], P(None, 'chan'), may hold values from -0.1875 to 0.1875
- w_out: bfloat16 [1024, 1024], P('chan'), may hold values from -0.25 to 0.25
- pool_kernel: float32 [2, 27, 64], replicated, may hold values from -1.25 to 1.25
Outputs:
- block_out: bfloat16 [131072, 1024], P('tm', 'chan')
All inputs are finite; a program needn't handle non-finite values.
Results may differ from a plain program's by a relative error of at most 0.0053.
Values may be sent and summed in bfloat16 or wider, within the bound.
No kernel may reach another device: no remote copies, remote signals or barrier semaphores. Data moves between devices by JAX's collectives and lax.ppermute only.
A program may use at most 128 MiB of HBM per device.

v0:
```python
import functools
import math

import jax
import jax.numpy as jnp
import ml_dtypes
import numpy as np
from jax import lax
from jax.experimental import pallas as pl
from jax.experimental.pallas import tpu as pltpu
from jax.sharding import PartitionSpec as P

D = 1024
HDIM = 64
HH = 16
WW = 16
FRAME = HH * WW
POOL_ROWS = (HH // 4) * (WW // 4)
TAP_ROWS = FRAME // 2
RING = 8
REACH = 6
TILE = 256
CHUNKS = (1, 2, 3, 2)
EPSILON = 1e-06
MB = 1024 * 1024


def tap_order():
    wanted = []
    for second in range(3):
        for third in range(3):
            for row in range(HH // 4):
                for col in range(WW // 4):
                    i, j = 4 * row - 1 + second, 4 * col - 1 + third
                    wanted.append(i * WW + j if i >= 0 and j >= 0 else -1)
    used = sorted(set(t for t in wanted if t >= 0))
    order = np.array(used + [t for t in range(FRAME) if t not in set(used)])
    place = np.argsort(order)
    return order, np.array([place[t] if t >= 0 else -1 for t in wanted])


ORDER, TAP_PLACE = tap_order()
TAP_GATHER = (TAP_PLACE[:, None] == np.arange(TAP_ROWS)[None, :]).astype(ml_dtypes.bfloat16)


def place_of(token):
    i, j = token // WW, token % WW
    rows_before, cols_before = i - (i + 1) // 4, j - (j + 1) // 4
    row_used = (i % 4 != 2) & (i != HH - 1)
    col_used = (j % 4 != 2) & (j != WW - 1)
    side = HH - 1 - HH // 4
    used_before = rows_before * side + jnp.where(row_used, cols_before, 0)
    return jnp.where(row_used & col_used, used_before, side * side + token - used_before)


def move_matrix(back):
    shape = (FRAME, FRAME)
    token = lax.broadcasted_iota(jnp.int32, shape, 0 if back else 1)
    place = lax.broadcasted_iota(jnp.int32, shape, 1 if back else 0)
    return jnp.where(place_of(token) == place, 1.0, 0.0).astype(jnp.bfloat16)


def vmem(count):
    return [pl.BlockSpec(memory_space=pltpu.VMEM)] * count


def params(limit=20):
    return pltpu.CompilerParams(vmem_limit_bytes=limit * MB)


def cost(flops, moved, exps=0):
    return pl.CostEstimate(flops=int(flops), bytes_accessed=int(moved), transcendentals=int(exps))


def dot(a, b):
    return jnp.dot(a, b, preferred_element_type=jnp.float32)


def arrange_kernel(
    tokens_hbm,
    w_out_hbm,
    wk_hbm,
    wv_hbm,
    wq_hbm,
    taps_ref,
    last_ref,
    across_ref,
    beside_ref,
    own_ref,
    key_value_ref,
    query_ref,
    tokens_ref,
    w_out_ref,
    frame_sems,
    w_sem,
    pack_sems,
):
    me = lax.axis_index("chan")
    frames = tokens_ref.shape[0] // FRAME
    count = frames * TAP_ROWS
    width = w_out_ref.shape[0]
    order = [frames - 1] + list(range(frames - 1))

    def frame_copy(f):
        rows = pl.ds(f * FRAME, FRAME)
        return pltpu.make_async_copy(tokens_hbm.at[rows, :], tokens_ref.at[rows, :], frame_sems.at[f])

    for f in order:
        frame_copy(f).start()
    w_copy = pltpu.make_async_copy(w_out_hbm, w_out_ref, w_sem)
    w_copy.start()
    copies = []
    for k in range(4):
        source = pl.ds(pl.multiple_of((me ^ k) * width, width), width)
        target = pl.ds(k * width, width)
        copies += [
            pltpu.make_async_copy(
                wk_hbm.at[source, :], key_value_ref.at[target, pl.ds(0, width)], pack_sems.at[3 * k]
            ),
            pltpu.make_async_copy(
                wv_hbm.at[source, :], key_value_ref.at[target, pl.ds(width, width)], pack_sems.at[3 * k + 1]
            ),
            pltpu.make_async_copy(wq_hbm.at[source, :], query_ref.at[target, :], pack_sems.at[3 * k + 2]),
        ]
    for copy in copies:
        copy.start()
    gather = move_matrix(False)
    for f in order:
        frame_copy(f).wait()
        moved = dot(gather, tokens_ref[f * FRAME : (f + 1) * FRAME, :]).astype(jnp.bfloat16)
        taps_ref[f * TAP_ROWS : (f + 1) * TAP_ROWS, :] = moved[:TAP_ROWS]
        if f == frames - 1:
            last_ref[...] = moved[:TAP_ROWS]
        across_ref[f * TAP_ROWS : (f + 1) * TAP_ROWS, :] = moved[TAP_ROWS:]
        beside_ref[f * TAP_ROWS : (f + 1) * TAP_ROWS, :] = moved[TAP_ROWS:]
    w_copy.wait()

    def columns(k):
        return w_out_ref[:, pl.ds(pl.multiple_of((me ^ k) * width, width), width)]

    own_ref[...] = columns(0)
    beside_ref[count:, :] = columns(1)
    across_ref[count : count + width, :] = columns(2)
    across_ref[count + width :, :] = columns(3)
    for copy in copies:
        copy.wait()


def project(pieces, start, count, weights):
    rows = jnp.concatenate([piece[start : start + count, :] for piece in pieces], axis=1)
    return dot(rows, weights).astype(jnp.bfloat16)


def weigh(slabs, taps, first):
    total = None
    for q in range(9):
        term = slabs[q * POOL_ROWS : (q + 1) * POOL_ROWS] * taps[9 * first + q : 9 * first + q + 1, :]
        total = term if total is None else total + term
    return total


def group_mean(rows, averaging):
    high = rows.astype(jnp.bfloat16)
    rest = rows - high.astype(jnp.float32)
    middle = rest.astype(jnp.bfloat16)
    low = (rest - middle.astype(jnp.float32)).astype(jnp.bfloat16)
    return dot(high, averaging) + dot(middle, averaging) + dot(low, averaging)


def pool_kernel_body(a0, a1, a2, a3, l0, l1, l2, l3, weights_ref, taps_ref, spread_ref, out_ref):
    width = weights_ref.shape[1] // 2
    lane = lax.broadcasted_iota(jnp.int32, (width, width), 1) // HDIM
    row = lax.broadcasted_iota(jnp.int32, (width, width), 0) // HDIM
    averaging = jnp.where(lane == row, 1.0 / HDIM, 0.0).astype(jnp.bfloat16)
    frames = a0.shape[0] // TAP_ROWS
    pooled_frames = frames // 2
    weights = weights_ref[...]
    taps = taps_ref[...]
    spread = spread_ref[...]
    sums = [None] * pooled_frames
    sums[0] = weigh(dot(spread, project((l0, l1, l2, l3), 0, TAP_ROWS, weights)), taps, 0)
    for f in range(frames):
        slabs = dot(spread, project((a0, a1, a2, a3), f * TAP_ROWS, TAP_ROWS, weights))
        t = f // 2
        part = weigh(slabs, taps, 1 + f % 2)
        sums[t] = part if sums[t] is None else sums[t] + part
        if f % 2 == 1 and t + 1 < pooled_frames:
            sums[t + 1] = weigh(slabs, taps, 0)
    pooled = jnp.concatenate(sums, axis=0)
    for side in range(2):
        lanes = slice(side * width, (side + 1) * width)
        center = pooled[:, lanes] - group_mean(pooled[:, lanes], averaging)
        spread_rows = group_mean(center * center, averaging)
        normal = (center * lax.rsqrt(spread_rows + EPSILON)).astype(jnp.bfloat16)
        for copy in range(out_ref.shape[0]):
            out_ref[copy, :, lanes] = normal


def tap_query_kernel(a0, a1, a2, a3, wq_ref, came_ref, after_ref, q_ref, *parts):
    del after_ref
    step = 2 * FRAME
    for start in range(0, q_ref.shape[0], step):
        q_ref[start : start + step, :] = project((a0, a1, a2, a3), start, step, wq_ref[...])
    at = 0
    for part in parts:
        part[...] = came_ref[at : at + part.shape[0], :]
        at += part.shape[0]


def query_kernel(q_ref, b0, b1, b2, c0, c1, wq_ref, *rest):
    outs, both = rest[:-1], rest[-1]
    frames = q_ref.shape[0] // TAP_ROWS
    back = move_matrix(True)
    places = [(ref, start) for ref in outs for start in range(0, ref.shape[0], FRAME)]
    far = c0.shape[0]
    for f in range(frames):
        at = f * TAP_ROWS
        both[f % 2, :TAP_ROWS, :] = q_ref[at : at + TAP_ROWS, :]
        c = c0 if at < far else c1
        pieces = [piece[at : at + TAP_ROWS, :] for piece in (b0, b1, b2)] + [c[at % far : at % far + TAP_ROWS, :]]
        others = dot(jnp.concatenate(pieces, axis=1), wq_ref[...])
        both[f % 2, TAP_ROWS:, :] = others.astype(jnp.bfloat16)
        ref, start = places[f]
        ref[start : start + FRAME, :] = dot(back, both[f % 2]).astype(jnp.bfloat16)


def ends_kernel(ring_ref, head_ref, tail_ref):
    edge = head_ref.shape[0]
    head_ref[...] = ring_ref[:edge, :]
    tail_ref[...] = ring_ref[ring_ref.shape[0] - edge :, :]


def attend_kernel(q_ref, before_ref, here_ref, after_ref, *rest):
    out_ref, window, keys, values = rest[-4:]
    width = q_ref.shape[1]
    heads = width // HDIM
    block = here_ref.shape[0] // RING
    count = keys.shape[1]
    z = lax.rem(lax.axis_index("tm"), RING)

    n = before_ref.shape[0]
    m = here_ref.shape[0]
    window[:n, :] = before_ref[...]
    window[n : n + m, :] = here_ref[...]
    window[n + m :, :] = after_ref[...]
    rows = window[pl.ds(pl.multiple_of(z * block, block), count), :]
    head = lax.broadcasted_iota(jnp.int32, (count, width), 1) // HDIM
    k = rows[:, :width].astype(jnp.float32) * (1.0 / math.sqrt(HDIM))
    v = rows[:, width:].astype(jnp.float32)
    for h in range(heads):
        keys[h] = jnp.where(head == h, k, 0.0).astype(jnp.bfloat16)
        values[h] = jnp.where(head == h, v, 0.0).astype(jnp.bfloat16)

    q = q_ref[...]
    total = q.astype(jnp.float32)
    for h in range(heads):
        scores = lax.dot_general(q, keys[h], (((1,), (1,)), ((), ())), preferred_element_type=jnp.float32)
        top = jnp.max(scores, axis=-1, keepdims=True)
        weighted = jnp.exp(scores - top)
        summed = jnp.sum(weighted, axis=-1, keepdims=True)
        total = total + dot(weighted.astype(jnp.bfloat16), values[h]) * (1.0 / summed)
    out_ref[...] = total.astype(jnp.bfloat16)


def out_kernel(a0, a1, a2, a3, w0, w1, w2, w3, tokens_ref, *rest):
    out_ref, done_ref = rest[-2:]
    done_ref[...] = jnp.zeros_like(done_ref)
    total = tokens_ref[...].astype(jnp.float32)
    acc = dot(a0[...], w0[...])
    for a, w in ((a1, w1), (a2, w2), (a3, w3)):
        acc = acc + dot(a[...], w[...])
    out_ref[...] = (total + acc).astype(jnp.bfloat16)


def swap(array, k):
    return lax.ppermute(array, "chan", [(i, i ^ k) for i in range(4)])


def per_device(tokens, w_query, w_key, w_value, w_out, pool_kernel):
    rows, width = tokens.shape
    frames = rows // FRAME
    devices = lax.axis_size("tm")
    bf16 = jnp.bfloat16
    tap_gather = jnp.asarray(TAP_GATHER)
    taps = jnp.concatenate(
        [jnp.tile(pool_kernel[0], (1, width // HDIM)), jnp.tile(pool_kernel[1], (1, width // HDIM))], axis=1
    )
    anywhere = pl.BlockSpec(memory_space=pl.ANY)

    hbm = pl.BlockSpec(memory_space=pltpu.HBM)
    half = frames * TAP_ROWS
    body, last, rest_across, rest_beside, w_own, key_value_weights, query_weights = pl.pallas_call(
        arrange_kernel,
        out_shape=(
            jax.ShapeDtypeStruct((half, width), bf16),
            jax.ShapeDtypeStruct((TAP_ROWS, width), bf16),
            jax.ShapeDtypeStruct((half + 2 * width, width), bf16),
            jax.ShapeDtypeStruct((half + width, width), bf16),
            jax.ShapeDtypeStruct((width, width), bf16),
            jax.ShapeDtypeStruct((D, 2 * width), bf16),
            jax.ShapeDtypeStruct((D, width), bf16),
        ),
        in_specs=[hbm] * 5,
        out_specs=tuple(vmem(5) + [anywhere, anywhere]),
        scratch_shapes=[
            pltpu.VMEM((rows, width), bf16),
            pltpu.VMEM((width, D), bf16),
            pltpu.SemaphoreType.DMA((frames,)),
            pltpu.SemaphoreType.DMA,
            pltpu.SemaphoreType.DMA((12,)),
        ],
        compiler_params=params(60),
        cost_estimate=cost(2 * rows * FRAME * width, 4 * rows * width),
        name="arrange",
    )(tokens, w_out, w_key, w_value, w_query)
    last = lax.ppermute(last, "tm", [(i, (i + 1) % devices) for i in range(devices)])

    last_across = swap(last, 2)
    body_across, last_across = lax.optimization_barrier((swap(body, 2), last_across))
    body_pieces = (body, swap(body, 1), body_across, swap(body_across, 1))
    last_pieces = (last, swap(last, 1), last_across, swap(last_across, 1))
    rest_later, last_came = lax.optimization_barrier((rest_across, last_pieces[2]))
    last_pieces = (*last_pieces[:2], last_came, last_pieces[3])
    from_chip = swap(rest_later, 2)
    from_core = swap(rest_beside, 1)

    block = pl.pallas_call(
        pool_kernel_body,
        out_shape=jax.ShapeDtypeStruct((RING, frames // 2 * POOL_ROWS, 2 * width), bf16),
        in_specs=vmem(11),
        out_specs=vmem(1)[0],
        compiler_params=params(),
        cost_estimate=cost(2 * frames * TAP_ROWS * D * 2 * width, 8 * rows * width),
        name="pool",
    )(*body_pieces, *last_pieces, key_value_weights, taps, tap_gather)

    block_rows = block.shape[1]
    rings = [[RING * r + z for z in range(RING)] for r in range(devices // RING)]
    ring = lax.all_to_all(block, "tm", 0, 0, axis_index_groups=rings).reshape(RING * block_rows, 2 * width)
    edge = (RING - 2) * block_rows
    head, tail = pl.pallas_call(
        ends_kernel,
        out_shape=(jax.ShapeDtypeStruct((edge, 2 * width), bf16), jax.ShapeDtypeStruct((edge, 2 * width), bf16)),
        in_specs=vmem(1),
        out_specs=tuple(vmem(2)),
        compiler_params=params(),
        cost_estimate=cost(0, 8 * edge * width),
        name="ends",
    )(ring)
    before = lax.ppermute(tail, "tm", [(i, (i + RING) % devices) for i in range(devices)])
    after = lax.ppermute(head, "tm", [((i + RING) % devices, i) for i in range(devices)])
    tap_queries, *onward = pl.pallas_call(
        tap_query_kernel,
        out_shape=tuple(jax.ShapeDtypeStruct((n, width), bf16) for n in (half, half // 2, half // 2, 2 * width)),
        in_specs=vmem(6) + [anywhere],
        out_specs=tuple(vmem(4)),
        compiler_params=params(),
        cost_estimate=cost(0, 0),
        name="tap_query",
    )(*body_pieces, query_weights, from_chip, ring)
    from_far = [swap(piece, 1) for piece in onward]

    queries = pl.pallas_call(
        query_kernel,
        out_shape=tuple(jax.ShapeDtypeStruct((n * TILE, width), bf16) for n in CHUNKS),
        in_specs=vmem(7),
        out_specs=tuple(vmem(len(CHUNKS))),
        scratch_shapes=[pltpu.VMEM((2, FRAME, width), bf16)],
        compiler_params=params(),
        cost_estimate=cost(0, 0),
        name="query",
    )(
        tap_queries,
        rest_across,
        from_core,
        from_chip,
        from_far[0],
        from_far[1],
        query_weights,
    )

    count = (2 * REACH + 1) * block_rows
    heads = width // HDIM
    starts = [sum(CHUNKS[:i]) for i in range(len(CHUNKS))]
    first = half // width
    attended = []
    came = []
    marks = []
    result = None

    def attend(i):
        chunk = CHUNKS[i] * TILE
        waited = attended[-1:] + (marks[-1:] if i == 3 else []) + (came[i - 2 : i - 1] if i >= 2 else [])
        out = pl.pallas_call(
            attend_kernel,
            out_shape=jax.ShapeDtypeStruct((chunk, width), bf16),
            in_specs=vmem(4) + [anywhere] * len(waited),
            out_specs=vmem(1)[0],
            scratch_shapes=[
                pltpu.VMEM((2 * edge + ring.shape[0], 2 * width), bf16),
                pltpu.VMEM((heads, count, width), bf16),
                pltpu.VMEM((heads, count, width), bf16),
            ],
            compiler_params=params(30),
            cost_estimate=cost(0, 0),
            name=f"attend{i}",
        )(queries[i], before, ring, after, *waited)
        attended.append(out)
        came.append(swap(out, 2))
        return out, swap(out, 1), came[-1]

    def finish(i, pieces, result):
        own, beside, across = pieces[i]
        extra = () if result is None else (result,)
        if i + 2 < len(CHUNKS):
            onward, later = lax.optimization_barrier((across, pieces[i + 2][0]))
            pieces[i + 2] = (later, *pieces[i + 2][1:])
        else:
            onward, later = lax.optimization_barrier((across, marks[i - 1]))
            extra = (*extra, later)
        start, tiles = starts[i], CHUNKS[i]
        result, mark = pl.pallas_call(
            out_kernel,
            grid=(tiles,),
            out_shape=(jax.ShapeDtypeStruct((rows, width), bf16), jax.ShapeDtypeStruct((8, 128), jnp.float32)),
            in_specs=[pl.BlockSpec((TILE, width), lambda s: (s, 0))] * 4
            + [pl.BlockSpec((width, width), lambda s, at=at: (at, 0)) for at in (0, first, first, 1)]
            + [pl.BlockSpec((TILE, width), lambda s: (start + s, 0))]
            + [anywhere] * len(extra),
            out_specs=(
                pl.BlockSpec((TILE, width), lambda s: (start + s, 0)),
                pl.BlockSpec((8, 128), lambda s: (0, 0)),
            ),
            input_output_aliases={9: 0} if extra else {},
            compiler_params=params(),
            cost_estimate=cost(0, 0),
            name=f"out{i}",
        )(own, beside, across, swap(onward, 1), w_own, from_core, from_chip, from_far[2], tokens, *extra)
        marks.append(mark)
        return result

    pieces = [attend(i) for i in range(3)]
    for i in range(len(CHUNKS)):
        result = finish(i, pieces, result)
        if i + 3 < len(CHUNKS):
            pieces.append(attend(i + 3))
    return result


def solution(mesh):
    return jax.shard_map(
        per_device,
        mesh=mesh,
        in_specs=(
            P("tm", "chan"),
            P(None, "chan"),
            P(None, "chan"),
            P(None, "chan"),
            P("chan", None),
            P(),
        ),
        out_specs=P("tm", "chan"),
        check_vma=False,
    )
```

profile of v0, /device:TPU:25, one launch (start us, length us, event | category | flops | bytes accessed | tf_op | source)
XLA Modules:
  0.0 155.2 jit_solution(17352830701410840735)
XLA Ops:
  0.0 50.3 %arrange.1 = (bf16[1024,256]{1,0:T(8,128)(2,1)}, bf16[128,256]{1,0:T(8,128)(2,1)}, bf16[1536,256]{1,0:T(8,128)(2,1)}, bf16[1280,256]{1,0:T(8,128)(2,1)}, bf16[25...) custom-call(bf16[2048,256]{1,0:T(8,128)(2,1)} %tokens_ref.7, bf16[256,1024]{1,0:T(8,128)(2,1)} %w_out_hbm.1, ...), custom_call_target="tpu_custom_call" | custom-call | flops 268435456 | bytes 2097152 | tf_op jit(solution)/shard_map/arrange/pallas_call | solution.py:292
  50.3 1.3 collective-permute-start.1
  51.6 1.6 %collective-permute-start.2 = (bf16[128,256]{1,0:T(8,128)(2,1)}, bf16[128,256]{1,0:T(8,128)(2,1)S(1)}, u32[]{:S(2)}, u32[]{:S(2)}) collective-permute-start(bf16[128,256]{1,0:T(8,128)(2,1)} %get-tuple-element.42), channel_id=1, source_target_pairs={{0,4},{4,8},{8,12},{12,16},{16,20},{20,24},{24,28},{28,32},{32,36}... | collective-permute-start | bytes 196616 | tf_op jit(solution)/shard_map/ppermute | solution.py:316
  53.3 6.0 %collective-permute-done.2.l0 = bf16[128,256]{1,0:T(8,128)(2,1)S(1)} collective-permute-done((bf16[128,256]{1,0:T(8,128)(2,1)}, bf16[128,256]{1,0:T(8,128)(2,1)S(1)}, u32[]{:S(2)}, u32[]{:S(2)}) %collective-permute-start.2) | collective-permute-done | bytes 65568 | tf_op jit(solution)/shard_map/ppermute | solution.py:316
  59.2 0.3 collective-permute-start.3
  59.5 2.1 %collective-permute-start = (bf16[1024,256]{1,0:T(8,128)(2,1)}, bf16[1024,256]{1,0:T(8,128)(2,1)S(1)}, u32[]{:S(2)}, u32[]{:S(2)}) collective-permute-start(bf16[1024,256]{1,0:T(8,128)(2,1)} %get-tuple-element.41.a0), channel_id=1, source_target_pairs={{0,1},{1,0},{2,3},{3,2},{4,5},{5,4},{6,7},{7,6},{8,9},{9,8},{10,11... | collective-permute-start | bytes 1572872 | tf_op jit(solution)/shard_map/ppermute | solution.py:276
  61.6 4.6 %collective-permute-done.3.l2 = bf16[128,256]{1,0:T(8,128)(2,1)S(1)} collective-permute-done((bf16[128,256]{1,0:T(8,128)(2,1)S(1)}, bf16[128,256]{1,0:T(8,128)(2,1)S(1)}, u32[]{:S(2)}, u32[]{:S(2)}) %collective-permute-start.3) | collective-permute-done | bytes 65568 | tf_op jit(solution)/shard_map/ppermute | solution.py:276
  66.2 0.0 collective-permute-done.1.a2
  66.2 1.5 collective-permute-start.4
  67.8 0.1 tile.22
  67.9 0.1 tile.25
  68.0 0.1 collective-permute-start.6
  68.1 0.5 collective-permute-start.7
  68.6 0.8 collective-permute-done.6.l1
  69.4 0.1 collective-permute-done.7.l3
  69.6 0.0 copy-start.6
  69.6 1.4 copy-done.6
  71.0 0.8 copy-done.9
  71.8 0.8 copy-done.11
  72.7 4.3 %pool.1 = bf16[8,64,512]{2,1,0:T(8,128)(2,1)} custom-call(bf16[1024,256]{1,0:T(8,128)(2,1)S(1)} %copy-done.1, bf16[1024,256]{1,0:T(8,128)(2,1)S(1)} %collective-permute-done.a1, bf16[1024,256]{1,0:T(8,128)(2,1)S(1)} %collective-permute-done.1.a2, bf16[1024,256]{1,0:T(8,128)(2,1)S(1)} %collective-permute-done.4.a3, bf16[128,256]{1,0:T(8,128)(2,1)S(1)} %copy-done.9, ...), custom_call_target="tpu_custom_call" | custom-call | flops 1073741824 | bytes 4194304 | tf_op jit(solution)/shard_map/pool/pallas_call | solution.py:327
  77.0 6.8 %all-to-all-start = ((bf16[8,64,512]{2,1,0:T(8,128)(2,1)}), bf16[8,64,512]{2,1,0:T(8,128)(2,1)S(1)}, u32[]{:S(2)}, u32[]{:S(2)}) async-start(bf16[8,64,512]{2,1,0:T(8,128)(2,1)} %pool.1), calls=%async_computation | async-start | bytes 1048576 | tf_op jit(solution)/shard_map/all_to_all | solution.py:339
  83.8 1.2 collective-permute-start.5
  85.0 0.9 collective-permute-start.8
  85.9 15.8 %all-to-all-done = bf16[8,64,512]{2,1,0:T(8,128)(2,1)S(1)} async-done(((bf16[8,64,512]{2,1,0:T(8,128)(2,1)}), bf16[8,64,512]{2,1,0:T(8,128)(2,1)S(1)}, u32[]{:S(2)}, u32[]{:S(2)}) %all-to-all-start) | async-done | bytes 524320 | tf_op jit(solution)/shard_map/all_to_all | solution.py:339
  101.7 0.1 ends.1
  101.8 2.5 %collective-permute-start.11 = (bf16[384,512]{1,0:T(8,128)(2,1)S(1)}, bf16[384,512]{1,0:T(8,128)(2,1)S(1)}, u32[]{:S(2)}, u32[]{:S(2)}) collective-permute-start(bf16[384,512]{1,0:T(8,128)(2,1)S(1)} %get-tuple-element.55), channel_id=1, source_target_pairs={{0,32},{4,36},{8,40},{12,44},{16,48},{20,52},{24,56},{28,60},{32,6... | collective-permute-start | bytes 1179656 | tf_op jit(solution)/shard_map/ppermute | solution.py:350
  104.3 0.0 collective-permute-start.12
  104.3 0.0 collective-permute-done.5.came_ref.b2.w2
  104.3 1.0 copy-done.4
  105.3 0.7 tap_query.1
  106.0 0.9 collective-permute-start.10
  106.9 0.3 collective-permute-start.9
  107.2 0.9 collective-permute-done.10.c1
  108.1 0.4 collective-permute-done.9.c0
  108.4 2.7 %query.1 = (bf16[256,256]{1,0:T(8,128)(2,1)S(1)}, bf16[512,256]{1,0:T(8,128)(2,1)S(1)}, bf16[768,256]{1,0:T(8,128)(2,1)S(1)}, bf16[512,256]{1,0:T(8,128)(2,1)S(1)}) custom-call(bf16[1024,256]{1,0:T(8,128)(2,1)S(1)} %get-tuple-element.50.q_ref, bf16[1536,256]{1,0:T(8,128)(2,1)S(1)} %copy-done.7, bf16[1280,256]{1,0:T(8,128)(2,1)S(1)} %collective-permute-done.8.b1.w1, ...), custom_call_target="tpu_custom_call" | custom-call | tf_op jit(solution)/shard_map/query/pallas_call | solution.py:363
  111.1 1.1 collective-permute-done.11.before_ref
  112.3 5.5 %collective-permute-done.12.after_ref = bf16[384,512]{1,0:T(8,128)(2,1)S(1)} collective-permute-done((bf16[384,512]{1,0:T(8,128)(2,1)S(1)}, bf16[384,512]{1,0:T(8,128)(2,1)S(1)}, u32[]{:S(2)}, u32[]{:S(2)}) %collective-permute-start.12) | collective-permute-done | bytes 393248 | tf_op jit(solution)/shard_map/ppermute | solution.py:351
  117.7 2.2 %attend0.1.rest_0_.a0 = bf16[256,256]{1,0:T(8,128)(2,1)S(1)} custom-call(bf16[256,256]{1,0:T(8,128)(2,1)S(1)} %get-tuple-element.57.q_ref, bf16[384,512]{1,0:T(8,128)(2,1)S(1)} %collective-permute-done.11.before_ref, bf16[512,512]{1,0:T(8,128)(2,1)S(1)} %bitcast.7, bf16[384,512]{1,0:T(8,128)(2,1)S(1)} %collective-permute-done.12.after_ref), custom_call_target="tpu_custom_call" | custom-call | tf_op jit(solution)/shard_map/attend0/pallas_call | solution.py:394
  120.0 0.4 collective-permute-start.14
  120.4 1.9 %collective-permute-start.17 = (bf16[512,256]{1,0:T(8,128)(2,1)S(1)}, bf16[512,256]{1,0:T(8,128)(2,1)S(1)}, u32[]{:S(2)}, u32[]{:S(2)}) collective-permute-start(bf16[512,256]{1,0:T(8,128)(2,1)S(1)} %get-tuple-element.62), channel_id=1, source_target_pairs={{0,1},{1,0},{2,3},{3,2},{4,5},{5,4},{6,7},{7,6},{8,9},{9,8},{10,11... | collective-permute-start | bytes 786440 | tf_op jit(solution)/shard_map/ppermute | solution.py:276
  122.3 3.5 %attend1.1.rest_0_.a0 = bf16[512,256]{1,0:T(8,128)(2,1)S(1)} custom-call(bf16[512,256]{1,0:T(8,128)(2,1)S(1)} %get-tuple-element.54.q_ref, bf16[384,512]{1,0:T(8,128)(2,1)S(1)} %collective-permute-done.11.before_ref, bf16[512,512]{1,0:T(8,128)(2,1)S(1)} %bitcast.8, bf16[384,512]{1,0:T(8,128)(2,1)S(1)} %collective-permute-done.12.after_ref, ...), custom_call_target="tpu_custom_call" | custom-call | tf_op jit(solution)/shard_map/attend1/pallas_call | solution.py:394
  125.8 1.2 collective-permute-start.13
  127.1 0.3 collective-permute-start.15
  127.4 4.8 %attend2.1.rest_0_.a0 = bf16[768,256]{1,0:T(8,128)(2,1)S(1)} custom-call(bf16[768,256]{1,0:T(8,128)(2,1)S(1)} %get-tuple-element.59.q_ref, bf16[384,512]{1,0:T(8,128)(2,1)S(1)} %collective-permute-done.11.before_ref, bf16[512,512]{1,0:T(8,128)(2,1)S(1)} %bitcast.9, bf16[384,512]{1,0:T(8,128)(2,1)S(1)} %collective-permute-done.12.after_ref, ...), custom_call_target="tpu_custom_call" | custom-call | tf_op jit(solution)/shard_map/attend2/pallas_call | solution.py:394
  132.2 0.3 collective-permute-start.16
  132.5 0.3 collective-permute-start.21
  132.8 0.6 collective-permute-start.22
  133.3 0.2 collective-permute-done.16.a3
  133.6 1.0 out0.1
  134.6 3.5 %attend3.1.a0 = bf16[512,256]{1,0:T(8,128)(2,1)S(1)} custom-call(bf16[512,256]{1,0:T(8,128)(2,1)S(1)} %get-tuple-element.58.q_ref, bf16[384,512]{1,0:T(8,128)(2,1)S(1)} %collective-permute-done.11.before_ref, bf16[512,512]{1,0:T(8,128)(2,1)S(1)} %bitcast.10, bf16[384,512]{1,0:T(8,128)(2,1)S(1)} %collective-permute-done.12.after_ref, ...), custom_call_target="tpu_custom_call" | custom-call | tf_op jit(solution)/shard_map/attend3/pallas_call | solution.py:394
  138.1 0.3 collective-permute-start.23
  138.4 0.3 collective-permute-start.20
  138.7 1.0 collective-permute-done.23.a3
  139.7 1.3 out1.1
  141.0 1.9 %collective-permute-done.21.a2 = bf16[768,256]{1,0:T(8,128)(2,1)S(1)} collective-permute-done((bf16[768,256]{1,0:T(8,128)(2,1)S(1)}, bf16[768,256]{1,0:T(8,128)(2,1)S(1)}, u32[]{:S(2)}, u32[]{:S(2)}) %collective-permute-start.21) | collective-permute-done | bytes 393248 | tf_op jit(solution)/shard_map/ppermute | solution.py:276
  142.9 1.1 collective-permute-start.24
  144.0 0.3 collective-permute-start.19
  144.3 0.3 collective-permute-start.18
  144.6 0.7 collective-permute-done.24.a3
  145.3 1.9 %out2.1 = (bf16[2048,256]{1,0:T(8,128)(2,1)}, f32[8,128]{1,0:T(8,128)S(1)}) custom-call(bf16[768,256]{1,0:T(8,128)(2,1)S(1)} %attend2.1.rest_0_.a0, bf16[768,256]{1,0:T(8,128)(2,1)S(1)} %collective-permute-done.20.a1, bf16[768,256]{1,0:T(8,128)(2,1)S(1)} %collective-permute-done.21.a2, ...), custom_call_target="tpu_custom_call", output_to_operand_aliasing={{0}: (9, {})} | custom-call | tf_op jit(solution)/shard_map/out2/pallas_call | solution.py:422
  147.3 4.7 %collective-permute-done.19.a2 = bf16[512,256]{1,0:T(8,128)(2,1)S(1)} collective-permute-done((bf16[512,256]{1,0:T(8,128)(2,1)S(1)}, bf16[512,256]{1,0:T(8,128)(2,1)S(1)}, u32[]{:S(2)}, u32[]{:S(2)}) %collective-permute-start.19) | collective-permute-done | bytes 262176 | tf_op jit(solution)/shard_map/ppermute | solution.py:276
  151.9 0.8 collective-permute-start.25
  152.7 1.2 collective-permute-done.25.a3
  153.9 1.3 out3.1
  (38 shorter events, 0.1 us)
Async XLA Ops:
  0.0 67.8 %copy-start.13 = (f32[2,27,64]{2,0,1:T(2,128)S(1)}, f32[2,27,64]{2,0,1:T(2,128)}, u32[]{:S(2)}) copy-start(f32[2,27,64]{2,0,1:T(2,128)} %param.12) | copy-start | bytes 41476
  50.3 19.2 %copy-start.1 = (bf16[1024,256]{1,0:T(8,128)(2,1)S(1)}, bf16[1024,256]{1,0:T(8,128)(2,1)}, u32[]{:S(2)}) copy-start(bf16[1024,256]{1,0:T(8,128)(2,1)} %get-tuple-element.41.a0) | copy-start | bytes 1572868
  50.3 15.9 %collective-permute-start.1 = (bf16[1024,256]{1,0:T(8,128)(2,1)}, bf16[1024,256]{1,0:T(8,128)(2,1)S(1)}, u32[]{:S(2)}, u32[]{:S(2)}) collective-permute-start(bf16[1024,256]{1,0:T(8,128)(2,1)} %get-tuple-element.41.a0), channel_id=1, source_target_pairs={{0,2},{1,3},{2,0},{3,1},{4,6},{5,7},{6,4},{7,5},{8,10},{9,11},{10,... | collective-permute-start | bytes 1572872 | tf_op jit(solution)/shard_map/ppermute | solution.py:276
  51.6 7.6 %collective-permute-start.2 = (bf16[128,256]{1,0:T(8,128)(2,1)}, bf16[128,256]{1,0:T(8,128)(2,1)S(1)}, u32[]{:S(2)}, u32[]{:S(2)}) collective-permute-start(bf16[128,256]{1,0:T(8,128)(2,1)} %get-tuple-element.42), channel_id=1, source_target_pairs={{0,4},{4,8},{8,12},{12,16},{16,20},{20,24},{24,28},{28,32},{32,36}... | collective-permute-start | bytes 196616 | tf_op jit(solution)/shard_map/ppermute | solution.py:316
  59.2 8.8 %copy-start.8 = (bf16[128,256]{1,0:T(8,128)(2,1)}, bf16[128,256]{1,0:T(8,128)(2,1)S(1)}, u32[]{:S(2)}) copy-start(bf16[128,256]{1,0:T(8,128)(2,1)S(1)} %collective-permute-done.2.l0) | copy-start | bytes 196612
  59.2 7.0 %collective-permute-start.3 = (bf16[128,256]{1,0:T(8,128)(2,1)S(1)}, bf16[128,256]{1,0:T(8,128)(2,1)S(1)}, u32[]{:S(2)}, u32[]{:S(2)}) collective-permute-start(bf16[128,256]{1,0:T(8,128)(2,1)S(1)} %collective-permute-done.2.l0), channel_id=1, source_target_pairs={{0,2},{1,3},{2,0},{3,1},{4,6},{5,7},{6,4},{7,5},{8,10},{9,11},{10,... | collective-permute-start | bytes 196616 | tf_op jit(solution)/shard_map/ppermute | solution.py:276
  59.5 9.9 %collective-permute-start = (bf16[1024,256]{1,0:T(8,128)(2,1)}, bf16[1024,256]{1,0:T(8,128)(2,1)S(1)}, u32[]{:S(2)}, u32[]{:S(2)}) collective-permute-start(bf16[1024,256]{1,0:T(8,128)(2,1)} %get-tuple-element.41.a0), channel_id=1, source_target_pairs={{0,1},{1,0},{2,3},{3,2},{4,5},{5,4},{6,7},{7,6},{8,9},{9,8},{10,11... | collective-permute-start | bytes 1572872 | tf_op jit(solution)/shard_map/ppermute | solution.py:276
  66.2 1.9 %copy-start.10 = (bf16[128,256]{1,0:T(8,128)(2,1)}, bf16[128,256]{1,0:T(8,128)(2,1)S(1)}, u32[]{:S(2)}) copy-start(bf16[128,256]{1,0:T(8,128)(2,1)S(1)} %collective-permute-done.3.l2) | copy-start | bytes 196612
  66.2 3.3 %collective-permute-start.4 = (bf16[1024,256]{1,0:T(8,128)(2,1)S(1)}, bf16[1024,256]{1,0:T(8,128)(2,1)S(1)}, u32[]{:S(2)}, u32[]{:S(2)}) collective-permute-start(bf16[1024,256]{1,0:T(8,128)(2,1)S(1)} %collective-permute-done.1.a2), channel_id=1, source_target_pairs={{0,1},{1,0},{2,3},{3,2},{4,5},{5,4},{6,7},{7,6},{8,9},{9,8},{10,11... | collective-permute-start | bytes 1572872 | tf_op jit(solution)/shard_map/ppermute | solution.py:276
  68.0 1.5 copy-start.12
  68.0 1.4 collective-permute-start.6
  68.1 1.4 collective-permute-start.7
  69.5 7.4 %copy-start.2 = (bf16[1024,256]{1,0:T(8,128)(2,1)}, bf16[1024,256]{1,0:T(8,128)(2,1)S(1)}, u32[]{:S(2)}) copy-start(bf16[1024,256]{1,0:T(8,128)(2,1)S(1)} %collective-permute-done.4.a3) | copy-start | bytes 1572868
  69.6 1.4 copy-start.6
  71.0 0.8 copy-start.9
  71.8 0.8 copy-start.11
  77.0 24.7 %all-to-all-start = ((bf16[8,64,512]{2,1,0:T(8,128)(2,1)}), bf16[8,64,512]{2,1,0:T(8,128)(2,1)S(1)}, u32[]{:S(2)}, u32[]{:S(2)}) async-start(bf16[8,64,512]{2,1,0:T(8,128)(2,1)} %pool.1), calls=%async_computation | async-start | bytes 1048576 | tf_op jit(solution)/shard_map/all_to_all | solution.py:339
  83.8 20.5 %collective-permute-start.5 = (bf16[1536,256]{1,0:T(8,128)(2,1)}, bf16[1536,256]{1,0:T(8,128)(2,1)S(1)}, u32[]{:S(2)}, u32[]{:S(2)}) collective-permute-start(bf16[1536,256]{1,0:T(8,128)(2,1)} %get-tuple-element.47.b0), channel_id=1, source_target_pairs={{0,2},{1,3},{2,0},{3,1},{4,6},{5,7},{6,4},{7,5},{8,10},{9,11},{10,... | collective-permute-start | bytes 2359304 | tf_op jit(solution)/shard_map/ppermute | solution.py:276
  85.0 22.2 %collective-permute-start.8 = (bf16[1280,256]{1,0:T(8,128)(2,1)}, bf16[1280,256]{1,0:T(8,128)(2,1)S(1)}, u32[]{:S(2)}, u32[]{:S(2)}) collective-permute-start(bf16[1280,256]{1,0:T(8,128)(2,1)} %get-tuple-element.51), channel_id=1, source_target_pairs={{0,1},{1,0},{2,3},{3,2},{4,5},{5,4},{6,7},{7,6},{8,9},{9,8},{10,11... | collective-permute-start | bytes 1966088 | tf_op jit(solution)/shard_map/ppermute | solution.py:276
  101.7 2.6 %copy-start.3 = (bf16[1024,256]{1,0:T(8,128)(2,1)S(1)}, bf16[1024,256]{1,0:T(8,128)(2,1)}, u32[]{:S(2)}) copy-start(bf16[1024,256]{1,0:T(8,128)(2,1)} %copy-done.2) | copy-start | bytes 1572868
  101.8 10.5 %collective-permute-start.11 = (bf16[384,512]{1,0:T(8,128)(2,1)S(1)}, bf16[384,512]{1,0:T(8,128)(2,1)S(1)}, u32[]{:S(2)}, u32[]{:S(2)}) collective-permute-start(bf16[384,512]{1,0:T(8,128)(2,1)S(1)} %get-tuple-element.55), channel_id=1, source_target_pairs={{0,32},{4,36},{8,40},{12,44},{16,48},{20,52},{24,56},{28,60},{32,6... | collective-permute-start | bytes 1179656 | tf_op jit(solution)/shard_map/ppermute | solution.py:350
  104.3 13.5 %collective-permute-start.12 = (bf16[384,512]{1,0:T(8,128)(2,1)S(1)}, bf16[384,512]{1,0:T(8,128)(2,1)S(1)}, u32[]{:S(2)}, u32[]{:S(2)}) collective-permute-start(bf16[384,512]{1,0:T(8,128)(2,1)S(1)} %get-tuple-element.56), channel_id=1, source_target_pairs={{32,0},{36,4},{40,8},{44,12},{48,16},{52,20},{56,24},{60,28},{64,3... | collective-permute-start | bytes 1179656 | tf_op jit(solution)/shard_map/ppermute | solution.py:351
  104.3 1.0 copy-start.4
  105.3 3.1 %copy-start.7 = (bf16[1536,256]{1,0:T(8,128)(2,1)S(1)}, bf16[1536,256]{1,0:T(8,128)(2,1)}, u32[]{:S(2)}) copy-start(bf16[1536,256]{1,0:T(8,128)(2,1)} %get-tuple-element.47.b0) | copy-start | bytes 2359300
  106.0 2.0 %collective-permute-start.10 = (bf16[512,256]{1,0:T(8,128)(2,1)S(1)}, bf16[512,256]{1,0:T(8,128)(2,1)S(1)}, u32[]{:S(2)}, u32[]{:S(2)}) collective-permute-start(bf16[512,256]{1,0:T(8,128)(2,1)S(1)} %get-tuple-element.53), channel_id=1, source_target_pairs={{0,1},{1,0},{2,3},{3,2},{4,5},{5,4},{6,7},{7,6},{8,9},{9,8},{10,11... | collective-permute-start | bytes 786440 | tf_op jit(solution)/shard_map/ppermute | solution.py:276
  106.9 1.5 collective-permute-start.9
  120.0 7.4 %collective-permute-start.14 = (bf16[256,256]{1,0:T(8,128)(2,1)S(1)}, bf16[256,256]{1,0:T(8,128)(2,1)S(1)}, u32[]{:S(2)}, u32[]{:S(2)}) collective-permute-start(bf16[256,256]{1,0:T(8,128)(2,1)S(1)} %attend0.1.rest_0_.a0), channel_id=1, source_target_pairs={{0,2},{1,3},{2,0},{3,1},{4,6},{5,7},{6,4},{7,5},{8,10},{9,11},{10,... | collective-permute-start | bytes 393224 | tf_op jit(solution)/shard_map/ppermute | solution.py:276
  120.4 12.4 %collective-permute-start.17 = (bf16[512,256]{1,0:T(8,128)(2,1)S(1)}, bf16[512,256]{1,0:T(8,128)(2,1)S(1)}, u32[]{:S(2)}, u32[]{:S(2)}) collective-permute-start(bf16[512,256]{1,0:T(8,128)(2,1)S(1)} %get-tuple-element.62), channel_id=1, source_target_pairs={{0,1},{1,0},{2,3},{3,2},{4,5},{5,4},{6,7},{7,6},{8,9},{9,8},{10,11... | collective-permute-start | bytes 786440 | tf_op jit(solution)/shard_map/ppermute | solution.py:276
  125.8 8.8 %collective-permute-start.13 = (bf16[512,256]{1,0:T(8,128)(2,1)S(1)}, bf16[512,256]{1,0:T(8,128)(2,1)S(1)}, u32[]{:S(2)}, u32[]{:S(2)}) collective-permute-start(bf16[512,256]{1,0:T(8,128)(2,1)S(1)} %attend1.1.rest_0_.a0), channel_id=1, source_target_pairs={{0,2},{1,3},{2,0},{3,1},{4,6},{5,7},{6,4},{7,5},{8,10},{9,11},{10,... | collective-permute-start | bytes 786440 | tf_op jit(solution)/shard_map/ppermute | solution.py:276
  127.1 6.3 %collective-permute-start.15 = (bf16[256,256]{1,0:T(8,128)(2,1)S(1)}, bf16[256,256]{1,0:T(8,128)(2,1)S(1)}, u32[]{:S(2)}, u32[]{:S(2)}) collective-permute-start(bf16[256,256]{1,0:T(8,128)(2,1)S(1)} %attend0.1.rest_0_.a0), channel_id=1, source_target_pairs={{0,1},{1,0},{2,3},{3,2},{4,5},{5,4},{6,7},{7,6},{8,9},{9,8},{10,11... | collective-permute-start | bytes 393224 | tf_op jit(solution)/shard_map/ppermute | solution.py:276
  127.3 6.2 %copy-start = (bf16[2048,256]{1,0:T(8,128)(2,1)S(1)}, bf16[2048,256]{1,0:T(8,128)(2,1)}, u32[]{:S(2)}) copy-start(bf16[2048,256]{1,0:T(8,128)(2,1)} %tokens_ref.7) | copy-start | bytes 3145732
  127.3 6.2 %copy-start.5 = (bf16[256,256]{1,0:T(8,128)(2,1)S(1)}, bf16[256,256]{1,0:T(8,128)(2,1)}, u32[]{:S(2)}) copy-start(bf16[256,256]{1,0:T(8,128)(2,1)} %get-tuple-element.61.w0) | copy-start | bytes 393220
  132.2 1.4 collective-permute-start.16
  132.5 10.4 %collective-permute-start.21 = (bf16[768,256]{1,0:T(8,128)(2,1)S(1)}, bf16[768,256]{1,0:T(8,128)(2,1)S(1)}, u32[]{:S(2)}, u32[]{:S(2)}) collective-permute-start(bf16[768,256]{1,0:T(8,128)(2,1)S(1)} %attend2.1.rest_0_.a0), channel_id=1, source_target_pairs={{0,2},{1,3},{2,0},{3,1},{4,6},{5,7},{6,4},{7,5},{8,10},{9,11},{10,... | collective-permute-start | bytes 1179656 | tf_op jit(solution)/shard_map/ppermute | solution.py:276
  132.8 5.9 %collective-permute-start.22 = (bf16[512,256]{1,0:T(8,128)(2,1)S(1)}, bf16[512,256]{1,0:T(8,128)(2,1)S(1)}, u32[]{:S(2)}, u32[]{:S(2)}) collective-permute-start(bf16[512,256]{1,0:T(8,128)(2,1)S(1)} %attend1.1.rest_0_.a0), channel_id=1, source_target_pairs={{0,1},{1,0},{2,3},{3,2},{4,5},{5,4},{6,7},{7,6},{8,9},{9,8},{10,11... | collective-permute-start | bytes 786440 | tf_op jit(solution)/shard_map/ppermute | solution.py:276
  138.1 1.6 %collective-permute-start.23 = (bf16[512,256]{1,0:T(8,128)(2,1)S(1)}, bf16[512,256]{1,0:T(8,128)(2,1)S(1)}, u32[]{:S(2)}, u32[]{:S(2)}) collective-permute-start(bf16[512,256]{1,0:T(8,128)(2,1)S(1)} %collective-permute-done.13.rest_2_.a2), channel_id=1, source_target_pairs={{0,1},{1,0},{2,3},{3,2},{4,5},{5,4},{6,7},{7,6},{8,9},{9,8},{10,11... | collective-permute-start | bytes 786440 | tf_op jit(solution)/shard_map/ppermute | solution.py:276
  138.4 6.2 %collective-permute-start.20 = (bf16[768,256]{1,0:T(8,128)(2,1)S(1)}, bf16[768,256]{1,0:T(8,128)(2,1)S(1)}, u32[]{:S(2)}, u32[]{:S(2)}) collective-permute-start(bf16[768,256]{1,0:T(8,128)(2,1)S(1)} %attend2.1.rest_0_.a0), channel_id=1, source_target_pairs={{0,1},{1,0},{2,3},{3,2},{4,5},{5,4},{6,7},{7,6},{8,9},{9,8},{10,11... | collective-permute-start | bytes 1179656 | tf_op jit(solution)/shard_map/ppermute | solution.py:276
  142.9 2.5 %collective-permute-start.24 = (bf16[768,256]{1,0:T(8,128)(2,1)S(1)}, bf16[768,256]{1,0:T(8,128)(2,1)S(1)}, u32[]{:S(2)}, u32[]{:S(2)}) collective-permute-start(bf16[768,256]{1,0:T(8,128)(2,1)S(1)} %collective-permute-done.21.a2), channel_id=1, source_target_pairs={{0,1},{1,0},{2,3},{3,2},{4,5},{5,4},{6,7},{7,6},{8,9},{9,8},{10,11... | collective-permute-start | bytes 1179656 | tf_op jit(solution)/shard_map/ppermute | solution.py:276
  144.0 7.9 %collective-permute-start.19 = (bf16[512,256]{1,0:T(8,128)(2,1)S(1)}, bf16[512,256]{1,0:T(8,128)(2,1)S(1)}, u32[]{:S(2)}, u32[]{:S(2)}) collective-permute-start(bf16[512,256]{1,0:T(8,128)(2,1)S(1)} %attend3.1.a0), channel_id=1, source_target_pairs={{0,2},{1,3},{2,0},{3,1},{4,6},{5,7},{6,4},{7,5},{8,10},{9,11},{10,... | collective-permute-start | bytes 786440 | tf_op jit(solution)/shard_map/ppermute | solution.py:276
  144.3 8.4 %collective-permute-start.18 = (bf16[512,256]{1,0:T(8,128)(2,1)S(1)}, bf16[512,256]{1,0:T(8,128)(2,1)S(1)}, u32[]{:S(2)}, u32[]{:S(2)}) collective-permute-start(bf16[512,256]{1,0:T(8,128)(2,1)S(1)} %attend3.1.a0), channel_id=1, source_target_pairs={{0,1},{1,0},{2,3},{3,2},{4,5},{5,4},{6,7},{7,6},{8,9},{9,8},{10,11... | collective-permute-start | bytes 786440 | tf_op jit(solution)/shard_map/ppermute | solution.py:276
  151.9 1.9 %collective-permute-start.25 = (bf16[512,256]{1,0:T(8,128)(2,1)S(1)}, bf16[512,256]{1,0:T(8,128)(2,1)S(1)}, u32[]{:S(2)}, u32[]{:S(2)}) collective-permute-start(bf16[512,256]{1,0:T(8,128)(2,1)S(1)} %collective-permute-done.19.a2), channel_id=1, source_target_pairs={{0,1},{1,0},{2,3},{3,2},{4,5},{5,4},{6,7},{7,6},{8,9},{9,8},{10,11... | collective-permute-start | bytes 786440 | tf_op jit(solution)/shard_map/ppermute | solution.py:276
where the time goes:
time: 156 us; the launch traced here: 155 us
  Pallas kernels  77.5 us (50%)
  waiting for transfers between devices  44.9 us (29%)
  starting transfers between devices  28.1 us (18%)
  local copies, waits for them, and re-layouts  4.4 us (3%)
    pallas_call x1, Pallas kernels, per_device(): pl.pallas_call(arrange_kernel, out_shape=(jax.ShapeDtypeStruct((half, wid...  50.3 us
    ppermute x23, starting transfers between devices, swap(): return lax.ppermute(array, 'chan', [(i, i ^ k) for i in range(4)])  17.2 us
    ppermute x23, waiting for transfers between devices, swap(): return lax.ppermute(array, 'chan', [(i, i ^ k) for i in range(4)])  16.5 us
    all_to_all x1, waiting for transfers between devices, per_device(): lax.all_to_all(block, 'tm', 0, 0, axis_index_groups=rings)  15.8 us
    pallas_call x4, Pallas kernels, attend(): pl.pallas_call(attend_kernel, out_shape=jax.ShapeDtypeStruct((chunk, widt...  14 us
    all_to_all x1, starting transfers between devices, per_device(): lax.all_to_all(block, 'tm', 0, 0, axis_index_groups=rings)  6.78 us
    ppermute x1, waiting for transfers between devices, per_device(): lax.ppermute(last, 'tm', [(i, (i + 1) % devices) for i in range(devices)])  5.98 us
    ppermute x1, waiting for transfers between devices, per_device(): lax.ppermute(head, 'tm', [((i + RING) % devices, i) for i in range(device...  5.49 us
  transfers between devices with their start and end apart: 27, of which 15 were waited for; matrix products, arithmetic and copies ran while one was open for 0% of the time, Pallas kernels for 13%

commit v1 on v0

--- a/solution.py
+++ b/solution.py
@@ -20,7 +20,7 @@
 RING = 8
 REACH = 6
 TILE = 256
-CHUNKS = (1, 2, 3, 2)
+CHUNKS = (1, 2, 2, 3)
 EPSILON = 1e-06
 MB = 1024 * 1024
 
@@ -77,23 +77,7 @@
 
 
 def arrange_kernel(
-    tokens_hbm,
-    w_out_hbm,
-    wk_hbm,
-    wv_hbm,
-    wq_hbm,
-    taps_ref,
-    last_ref,
-    across_ref,
-    beside_ref,
-    own_ref,
-    key_value_ref,
-    query_ref,
-    tokens_ref,
-    w_out_ref,
-    frame_sems,
-    w_sem,
-    pack_sems,
+    tokens_hbm, w_out_hbm, taps_ref, last_ref, across_ref, beside_ref, own_ref, tokens_ref, w_out_ref, frame_sems, w_sem
 ):
     me = lax.axis_index("chan")
     frames = tokens_ref.shape[0] // FRAME
@@ -109,21 +93,6 @@
         frame_copy(f).start()
     w_copy = pltpu.make_async_copy(w_out_hbm, w_out_ref, w_sem)
     w_copy.start()
-    copies = []
-    for k in range(4):
-        source = pl.ds(pl.multiple_of((me ^ k) * width, width), width)
-        target = pl.ds(k * width, width)
-        copies += [
-            pltpu.make_async_copy(
-                wk_hbm.at[source, :], key_value_ref.at[target, pl.ds(0, width)], pack_sems.at[3 * k]
-            ),
-            pltpu.make_async_copy(
-                wv_hbm.at[source, :], key_value_ref.at[target, pl.ds(width, width)], pack_sems.at[3 * k + 1]
-            ),
-            pltpu.make_async_copy(wq_hbm.at[source, :], query_ref.at[target, :], pack_sems.at[3 * k + 2]),
-        ]
-    for copy in copies:
-        copy.start()
     gather = move_matrix(False)
     for f in order:
         frame_copy(f).wait()
@@ -142,6 +111,26 @@
     beside_ref[count:, :] = columns(1)
     across_ref[count : count + width, :] = columns(2)
     across_ref[count + width :, :] = columns(3)
+
+
+def pack_kernel(wk_hbm, wv_hbm, wq_hbm, key_value_ref, query_ref, sems):
+    me = lax.axis_index("chan")
+    width = query_ref.shape[1]
+    copies = []
+    for k in range(4):
+        source = pl.ds(pl.multiple_of((me ^ k) * width, width), width)
+        target = pl.ds(k * width, width)
+        copies += [
+            pltpu.make_async_copy(
+                wk_hbm.at[source, :], key_value_ref.at[target, pl.ds(0, width)], sems.at[3 * k]
+            ),
+            pltpu.make_async_copy(
+                wv_hbm.at[source, :], key_value_ref.at[target, pl.ds(width, width)], sems.at[3 * k + 1]
+            ),
+            pltpu.make_async_copy(wq_hbm.at[source, :], query_ref.at[target, :], sems.at[3 * k + 2]),
+        ]
+    for copy in copies:
+        copy.start()
     for copy in copies:
         copy.wait()
 
@@ -289,7 +278,7 @@
 
     hbm = pl.BlockSpec(memory_space=pltpu.HBM)
     half = frames * TAP_ROWS
-    body, last, rest_across, rest_beside, w_own, key_value_weights, query_weights = pl.pallas_call(
+    body, last, rest_across, rest_beside, w_own = pl.pallas_call(
         arrange_kernel,
         out_shape=(
             jax.ShapeDtypeStruct((half, width), bf16),
@@ -297,24 +286,32 @@
             jax.ShapeDtypeStruct((half + 2 * width, width), bf16),
             jax.ShapeDtypeStruct((half + width, width), bf16),
             jax.ShapeDtypeStruct((width, width), bf16),
-            jax.ShapeDtypeStruct((D, 2 * width), bf16),
-            jax.ShapeDtypeStruct((D, width), bf16),
         ),
-        in_specs=[hbm] * 5,
-        out_specs=tuple(vmem(5) + [anywhere, anywhere]),
+        in_specs=[hbm] * 2,
+        out_specs=tuple(vmem(5)),
         scratch_shapes=[
             pltpu.VMEM((rows, width), bf16),
             pltpu.VMEM((width, D), bf16),
             pltpu.SemaphoreType.DMA((frames,)),
             pltpu.SemaphoreType.DMA,
-            pltpu.SemaphoreType.DMA((12,)),
         ],
         compiler_params=params(60),
         cost_estimate=cost(2 * rows * FRAME * width, 4 * rows * width),
         name="arrange",
-    )(tokens, w_out, w_key, w_value, w_query)
+    )(tokens, w_out)
+    key_value_weights, query_weights = pl.pallas_call(
+        pack_kernel,
+        out_shape=(jax.ShapeDtypeStruct((D, 2 * width), bf16), jax.ShapeDtypeStruct((D, width), bf16)),
+        in_specs=[hbm] * 3,
+        out_specs=tuple(vmem(2)),
+        scratch_shapes=[pltpu.SemaphoreType.DMA((12,))],
+        compiler_params=params(8),
+        cost_estimate=cost(0, 12 * D * width),
+        name="pack",
+    )(w_key, w_value, w_query)
     last = lax.ppermute(last, "tm", [(i, (i + 1) % devices) for i in range(devices)])
 
+    last, key_value_weights = lax.optimization_barrier((last, key_value_weights))
     last_across = swap(last, 2)
     body_across, last_across = lax.optimization_barrier((swap(body, 2), last_across))
     body_pieces = (body, swap(body, 1), body_across, swap(body_across, 1))
@@ -412,9 +409,10 @@
     def finish(i, pieces, result):
         own, beside, across = pieces[i]
         extra = () if result is None else (result,)
-        if i + 2 < len(CHUNKS):
-            onward, later = lax.optimization_barrier((across, pieces[i + 2][0]))
-            pieces[i + 2] = (later, *pieces[i + 2][1:])
+        n = min(i + 2, len(CHUNKS) - 1)
+        if i < n:
+            onward, later = lax.optimization_barrier((across, pieces[n][0]))
+            pieces[n] = (later, *pieces[n][1:])
         else:
             onward, later = lax.optimization_barrier((across, marks[i - 1]))
             extra = (*extra, later)

time: 156 us -> 106 us (0.68)
  Pallas kernels: 77.5 us -> 32.4 us
  waiting for transfers between devices: 44.9 us -> 38.5 us
  starting transfers between devices: 28.1 us -> 30.3 us
    pallas_call x1, Pallas kernels: 50.3 us -> 4.22 us  [per_device(): pl.pallas_call(arrange_kernel, out_shape=(jax.ShapeDtypeStruct((half, wid...]
    ppermute x23, waiting for transfers between devices: 16.5 us -> 11.8 us  [swap(): return lax.ppermute(array, 'chan', [(i, i ^ k) for i in range(4)])]
    unnamed x28 -> x34, local copies, waits for them, and re-layouts: 4.16 us -> 1.9 us
    ppermute x23, starting transfers between devices: 17.2 us -> 19.4 us  [swap(): return lax.ppermute(array, 'chan', [(i, i ^ k) for i in range(4)])]
    ppermute x1, waiting for transfers between devices: 5.98 us -> 4.26 us  [per_device(): lax.ppermute(last, 'tm', [(i, (i + 1) % devices) for i in range(devices)])]
  transfers between devices with their start and end apart: 27 -> 27, of which waited for: 15 -> 14; matrix products, arithmetic and copies ran while one was open for 0% -> 2% of each run, Pallas kernels for 13% -> 19%
where the time goes in v1:
time: 106 us
  waiting for transfers between devices  38.5 us (36%)
  Pallas kernels  32.4 us (31%)
  starting transfers between devices  30.3 us (29%)
  local copies, waits for them, and re-layouts  3.34 us (3%)
    ppermute x23, starting transfers between devices, swap(): return lax.ppermute(array, 'chan', [(i, i ^ k) for i in range(4)])  19.4 us
    all_to_all x1, waiting for transfers between devices, per_device(): lax.all_to_all(block, 'tm', 0, 0, axis_index_groups=rings)  15.8 us
    pallas_call x4, Pallas kernels, attend(): pl.pallas_call(attend_kernel, out_shape=jax.ShapeDtypeStruct((chunk, widt...  14 us
    ppermute x23, waiting for transfers between devices, swap(): return lax.ppermute(array, 'chan', [(i, i ^ k) for i in range(4)])  11.8 us
    all_to_all x1, starting transfers between devices, per_device(): lax.all_to_all(block, 'tm', 0, 0, axis_index_groups=rings)  6.78 us
    ppermute x1, waiting for transfers between devices, per_device(): lax.ppermute(head, 'tm', [((i + RING) % devices, i) for i in range(device...  5.49 us
    pallas_call x4, Pallas kernels, finish(): pl.pallas_call(out_kernel, grid=(tiles,), out_shape=(jax.ShapeDtypeStruct...  5.47 us
    pallas_call x1, Pallas kernels, per_device(): pl.pallas_call(pool_kernel_body, out_shape=jax.ShapeDtypeStruct((RING, fr...  4.32 us
  transfers between devices with their start and end apart: 27, of which 14 were waited for; matrix products, arithmetic and copies ran while one was open for 2% of the time, Pallas kernels for 19%

profile of v1, /device:TPU:25, one launch (start us, length us, event | category | flops | bytes accessed | tf_op | source)
XLA Modules:
  0.0 105.5 jit_solution(15312358156768072785)
XLA Ops:
  0.0 4.2 %arrange.1 = (bf16[1024,256]{1,0:T(8,128)(2,1)}, bf16[128,256]{1,0:T(8,128)(2,1)}, bf16[1536,256]{1,0:T(8,128)(2,1)}, bf16[1280,256]{1,0:T(8,128)(2,1)}, bf16[256,256]{1,0:T(8,128)(2,1)}) custom-call(bf16[2048,256]{1,0:T(8,128)(2,1)} %tokens_ref.7, bf16[256,1024]{1,0:T(8,128)(2,1)} %w_out_hbm.1), custom_call_target="tpu_custom_call" | custom-call | flops 268435456 | bytes 2097152 | tf_op jit(solution)/shard_map/arrange/pallas_call | solution.py:281
  4.2 1.3 %collective-permute-start.1 = (bf16[1024,256]{1,0:T(8,128)(2,1)}, bf16[1024,256]{1,0:T(8,128)(2,1)S(1)}, u32[]{:S(2)}, u32[]{:S(2)}) collective-permute-start(bf16[1024,256]{1,0:T(8,128)(2,1)} %get-tuple-element.42.a0), channel_id=1, source_target_pairs={{0,2},{1,3},{2,0},{3,1},{4,6},{5,7},{6,4},{7,5},{8,10},{9,11},{10,... | collective-permute-start | bytes 1572872 | tf_op jit(solution)/shard_map/ppermute | solution.py:265
  5.5 1.6 %collective-permute-start.2 = (bf16[128,256]{1,0:T(8,128)(2,1)}, bf16[128,256]{1,0:T(8,128)(2,1)S(1)}, u32[]{:S(2)}, u32[]{:S(2)}) collective-permute-start(bf16[128,256]{1,0:T(8,128)(2,1)} %get-tuple-element.43), channel_id=1, source_target_pairs={{0,4},{4,8},{8,12},{12,16},{16,20},{20,24},{24,28},{28,32},{32,36}... | collective-permute-start | bytes 196616 | tf_op jit(solution)/shard_map/ppermute | solution.py:312
  7.2 0.9 pack.1
  8.1 0.8 copy-done.4
  8.9 4.3 %collective-permute-done.2.l0 = bf16[128,256]{1,0:T(8,128)(2,1)S(1)} collective-permute-done((bf16[128,256]{1,0:T(8,128)(2,1)}, bf16[128,256]{1,0:T(8,128)(2,1)S(1)}, u32[]{:S(2)}, u32[]{:S(2)}) %collective-permute-start.2) | collective-permute-done | bytes 65568 | tf_op jit(solution)/shard_map/ppermute | solution.py:312
  13.2 0.3 collective-permute-start.3
  13.4 2.1 %collective-permute-start = (bf16[1024,256]{1,0:T(8,128)(2,1)S(1)}, bf16[1024,256]{1,0:T(8,128)(2,1)S(1)}, u32[]{:S(2)}, u32[]{:S(2)}) collective-permute-start(bf16[1024,256]{1,0:T(8,128)(2,1)S(1)} %copy-done.1), channel_id=1, source_target_pairs={{0,1},{1,0},{2,3},{3,2},{4,5},{5,4},{6,7},{7,6},{8,9},{9,8},{10,11... | collective-permute-start | bytes 1572872 | tf_op jit(solution)/shard_map/ppermute | solution.py:265
  15.5 4.6 %collective-permute-done.3.l2 = bf16[128,256]{1,0:T(8,128)(2,1)S(1)} collective-permute-done((bf16[128,256]{1,0:T(8,128)(2,1)S(1)}, bf16[128,256]{1,0:T(8,128)(2,1)S(1)}, u32[]{:S(2)}, u32[]{:S(2)}) %collective-permute-start.3) | collective-permute-done | bytes 65568 | tf_op jit(solution)/shard_map/ppermute | solution.py:265
  20.1 0.0 collective-permute-done.1.a2
  20.1 1.5 %collective-permute-start.4 = (bf16[1024,256]{1,0:T(8,128)(2,1)S(1)}, bf16[1024,256]{1,0:T(8,128)(2,1)S(1)}, u32[]{:S(2)}, u32[]{:S(2)}) collective-permute-start(bf16[1024,256]{1,0:T(8,128)(2,1)S(1)} %collective-permute-done.1.a2), channel_id=1, source_target_pairs={{0,1},{1,0},{2,3},{3,2},{4,5},{5,4},{6,7},{7,6},{8,9},{9,8},{10,11... | collective-permute-start | bytes 1572872 | tf_op jit(solution)/shard_map/ppermute | solution.py:265
  21.8 0.7 tile.22
  22.5 0.0 copy-start.15
  22.5 0.7 tile.25
  23.2 0.0 collective-permute-start.6
  23.2 0.5 collective-permute-start.7
  23.7 0.8 pad_maximum_fusion.taps_ref
  24.5 0.0 collective-permute-done.6.l1
  24.5 0.1 collective-permute-done.7.l3
  24.6 0.0 collective-permute-done.4.a3
  24.6 4.3 %pool.1 = bf16[8,64,512]{2,1,0:T(8,128)(2,1)} custom-call(bf16[1024,256]{1,0:T(8,128)(2,1)S(1)} %copy-done.1, bf16[1024,256]{1,0:T(8,128)(2,1)S(1)} %collective-permute-done.a1, bf16[1024,256]{1,0:T(8,128)(2,1)S(1)} %collective-permute-done.1.a2, bf16[1024,256]{1,0:T(8,128)(2,1)S(1)} %collective-permute-done.4.a3, bf16[128,256]{1,0:T(8,128)(2,1)S(1)} %copy-done.12, ...), custom_call_target="tpu_custom_call" | custom-call | flops 1073741824 | bytes 4194304 | tf_op jit(solution)/shard_map/pool/pallas_call | solution.py:324
  28.9 6.8 %all-to-all-start = ((bf16[8,64,512]{2,1,0:T(8,128)(2,1)}), bf16[8,64,512]{2,1,0:T(8,128)(2,1)S(1)}, u32[]{:S(2)}, u32[]{:S(2)}) async-start(bf16[8,64,512]{2,1,0:T(8,128)(2,1)} %pool.1), calls=%async_computation | async-start | bytes 1048576 | tf_op jit(solution)/shard_map/all_to_all | solution.py:336
  35.7 1.2 %collective-permute-start.5 = (bf16[1536,256]{1,0:T(8,128)(2,1)}, bf16[1536,256]{1,0:T(8,128)(2,1)S(1)}, u32[]{:S(2)}, u32[]{:S(2)}) collective-permute-start(bf16[1536,256]{1,0:T(8,128)(2,1)} %get-tuple-element.50.b0), channel_id=1, source_target_pairs={{0,2},{1,3},{2,0},{3,1},{4,6},{5,7},{6,4},{7,5},{8,10},{9,11},{10,... | collective-permute-start | bytes 2359304 | tf_op jit(solution)/shard_map/ppermute | solution.py:265
  36.9 0.9 collective-permute-start.8
  37.9 15.8 %all-to-all-done = bf16[8,64,512]{2,1,0:T(8,128)(2,1)S(1)} async-done(((bf16[8,64,512]{2,1,0:T(8,128)(2,1)}), bf16[8,64,512]{2,1,0:T(8,128)(2,1)S(1)}, u32[]{:S(2)}, u32[]{:S(2)}) %all-to-all-start) | async-done | bytes 524320 | tf_op jit(solution)/shard_map/all_to_all | solution.py:336
  53.7 0.1 ends.1
  53.7 2.5 %collective-permute-start.11 = (bf16[384,512]{1,0:T(8,128)(2,1)S(1)}, bf16[384,512]{1,0:T(8,128)(2,1)S(1)}, u32[]{:S(2)}, u32[]{:S(2)}) collective-permute-start(bf16[384,512]{1,0:T(8,128)(2,1)S(1)} %get-tuple-element.58), channel_id=1, source_target_pairs={{0,32},{4,36},{8,40},{12,44},{16,48},{20,52},{24,56},{28,60},{32,6... | collective-permute-start | bytes 1179656 | tf_op jit(solution)/shard_map/ppermute | solution.py:347
  56.2 0.0 collective-permute-start.12
  56.2 0.0 collective-permute-done.5.came_ref.b2.w2
  56.2 1.0 copy-done.5
  57.3 0.7 tap_query.1
  58.0 0.9 collective-permute-start.10
  58.8 0.3 collective-permute-start.9
  59.1 0.9 collective-permute-done.10.c1
  60.0 0.4 collective-permute-done.9.c0
  60.4 2.7 %query.1 = (bf16[256,256]{1,0:T(8,128)(2,1)S(1)}, bf16[512,256]{1,0:T(8,128)(2,1)S(1)}, bf16[512,256]{1,0:T(8,128)(2,1)S(1)}, bf16[768,256]{1,0:T(8,128)(2,1)S(1)}) custom-call(bf16[1024,256]{1,0:T(8,128)(2,1)S(1)} %get-tuple-element.53.q_ref, bf16[1536,256]{1,0:T(8,128)(2,1)S(1)} %copy-done.7, bf16[1280,256]{1,0:T(8,128)(2,1)S(1)} %collective-permute-done.8.b1.w1, ...), custom_call_target="tpu_custom_call" | custom-call | tf_op jit(solution)/shard_map/query/pallas_call | solution.py:360
  63.1 1.1 %collective-permute-done.11.before_ref = bf16[384,512]{1,0:T(8,128)(2,1)S(1)} collective-permute-done((bf16[384,512]{1,0:T(8,128)(2,1)S(1)}, bf16[384,512]{1,0:T(8,128)(2,1)S(1)}, u32[]{:S(2)}, u32[]{:S(2)}) %collective-permute-start.11) | collective-permute-done | bytes 393248 | tf_op jit(solution)/shard_map/ppermute | solution.py:347
  64.2 5.5 %collective-permute-done.12.after_ref = bf16[384,512]{1,0:T(8,128)(2,1)S(1)} collective-permute-done((bf16[384,512]{1,0:T(8,128)(2,1)S(1)}, bf16[384,512]{1,0:T(8,128)(2,1)S(1)}, u32[]{:S(2)}, u32[]{:S(2)}) %collective-permute-start.12) | collective-permute-done | bytes 393248 | tf_op jit(solution)/shard_map/ppermute | solution.py:348
  69.7 2.2 %attend0.1.rest_0_.a0 = bf16[256,256]{1,0:T(8,128)(2,1)S(1)} custom-call(bf16[256,256]{1,0:T(8,128)(2,1)S(1)} %get-tuple-element.61.q_ref, bf16[384,512]{1,0:T(8,128)(2,1)S(1)} %collective-permute-done.11.before_ref, bf16[512,512]{1,0:T(8,128)(2,1)S(1)} %bitcast.7, bf16[384,512]{1,0:T(8,128)(2,1)S(1)} %collective-permute-done.12.after_ref), custom_call_target="tpu_custom_call" | custom-call | tf_op jit(solution)/shard_map/attend0/pallas_call | solution.py:391
  71.9 0.4 collective-permute-start.13
  72.3 1.9 %collective-permute-start.18 = (bf16[512,256]{1,0:T(8,128)(2,1)S(1)}, bf16[512,256]{1,0:T(8,128)(2,1)S(1)}, u32[]{:S(2)}, u32[]{:S(2)}) collective-permute-start(bf16[512,256]{1,0:T(8,128)(2,1)S(1)} %get-tuple-element.65), channel_id=1, source_target_pairs={{0,1},{1,0},{2,3},{3,2},{4,5},{5,4},{6,7},{7,6},{8,9},{9,8},{10,11... | collective-permute-start | bytes 786440 | tf_op jit(solution)/shard_map/ppermute | solution.py:265
  74.3 3.5 %attend1.1.rest_0_.a0 = bf16[512,256]{1,0:T(8,128)(2,1)S(1)} custom-call(bf16[512,256]{1,0:T(8,128)(2,1)S(1)} %get-tuple-element.60.q_ref, bf16[384,512]{1,0:T(8,128)(2,1)S(1)} %collective-permute-done.11.before_ref, bf16[512,512]{1,0:T(8,128)(2,1)S(1)} %bitcast.8, bf16[384,512]{1,0:T(8,128)(2,1)S(1)} %collective-permute-done.12.after_ref, ...), custom_call_target="tpu_custom_call" | custom-call | tf_op jit(solution)/shard_map/attend1/pallas_call | solution.py:391
  77.8 1.2 %collective-permute-start.15 = (bf16[512,256]{1,0:T(8,128)(2,1)S(1)}, bf16[512,256]{1,0:T(8,128)(2,1)S(1)}, u32[]{:S(2)}, u32[]{:S(2)}) collective-permute-start(bf16[512,256]{1,0:T(8,128)(2,1)S(1)} %attend1.1.rest_0_.a0), channel_id=1, source_target_pairs={{0,2},{1,3},{2,0},{3,1},{4,6},{5,7},{6,4},{7,5},{8,10},{9,11},{10,... | collective-permute-start | bytes 786440 | tf_op jit(solution)/shard_map/ppermute | solution.py:265
  79.0 0.3 collective-permute-start.16
  79.3 3.5 %attend2.1.rest_0_.a0 = bf16[512,256]{1,0:T(8,128)(2,1)S(1)} custom-call(bf16[512,256]{1,0:T(8,128)(2,1)S(1)} %get-tuple-element.57.q_ref, bf16[384,512]{1,0:T(8,128)(2,1)S(1)} %collective-permute-done.11.before_ref, bf16[512,512]{1,0:T(8,128)(2,1)S(1)} %bitcast.9, bf16[384,512]{1,0:T(8,128)(2,1)S(1)} %collective-permute-done.12.after_ref, ...), custom_call_target="tpu_custom_call" | custom-call | tf_op jit(solution)/shard_map/attend2/pallas_call | solution.py:391
  82.8 0.4 collective-permute-start.14
  83.2 0.5 collective-permute-start.17
  83.7 1.0 collective-permute-done.17.a3
  84.7 1.0 out0.1
  85.7 0.1 collective-permute-done.15.rest_2_.a2
  85.8 4.8 %attend3.1.a0 = bf16[768,256]{1,0:T(8,128)(2,1)S(1)} custom-call(bf16[768,256]{1,0:T(8,128)(2,1)S(1)} %get-tuple-element.62.q_ref, bf16[384,512]{1,0:T(8,128)(2,1)S(1)} %collective-permute-done.11.before_ref, bf16[512,512]{1,0:T(8,128)(2,1)S(1)} %bitcast.10, bf16[384,512]{1,0:T(8,128)(2,1)S(1)} %collective-permute-done.12.after_ref, ...), custom_call_target="tpu_custom_call" | custom-call | tf_op jit(solution)/shard_map/attend3/pallas_call | solution.py:391
  90.6 1.2 %collective-permute-start.20 = (bf16[768,256]{1,0:T(8,128)(2,1)S(1)}, bf16[768,256]{1,0:T(8,128)(2,1)S(1)}, u32[]{:S(2)}, u32[]{:S(2)}) collective-permute-start(bf16[768,256]{1,0:T(8,128)(2,1)S(1)} %attend3.1.a0), channel_id=1, source_target_pairs={{0,2},{1,3},{2,0},{3,1},{4,6},{5,7},{6,4},{7,5},{8,10},{9,11},{10,... | collective-permute-start | bytes 1179656 | tf_op jit(solution)/shard_map/ppermute | solution.py:265
  91.8 1.4 %collective-permute-start.23 = (bf16[512,256]{1,0:T(8,128)(2,1)S(1)}, bf16[512,256]{1,0:T(8,128)(2,1)S(1)}, u32[]{:S(2)}, u32[]{:S(2)}) collective-permute-start(bf16[512,256]{1,0:T(8,128)(2,1)S(1)} %attend1.1.rest_0_.a0), channel_id=1, source_target_pairs={{0,1},{1,0},{2,3},{3,2},{4,5},{5,4},{6,7},{7,6},{8,9},{9,8},{10,11... | collective-permute-start | bytes 786440 | tf_op jit(solution)/shard_map/ppermute | solution.py:265
  93.3 0.5 collective-permute-start.24
  93.8 0.0 collective-permute-start.22
  93.8 0.6 collective-permute-done.23.a1
  94.5 0.4 collective-permute-start.19
  94.8 0.4 collective-permute-done.24.a3
  95.2 1.3 %out1.1 = (bf16[2048,256]{1,0:T(8,128)(2,1)}, f32[8,128]{1,0:T(8,128)}) custom-call(bf16[512,256]{1,0:T(8,128)(2,1)S(1)} %attend1.1.rest_0_.a0, bf16[512,256]{1,0:T(8,128)(2,1)S(1)} %collective-permute-done.23.a1, bf16[512,256]{1,0:T(8,128)(2,1)S(1)} %collective-permute-done.15.rest_2_.a2, ...), custom_call_target="tpu_custom_call", output_to_operand_aliasing={{0}: (9, {})} | custom-call | tf_op jit(solution)/shard_map/out1/pallas_call | solution.py:420
  96.5 1.3 %out2.1 = (bf16[2048,256]{1,0:T(8,128)(2,1)}, f32[8,128]{1,0:T(8,128)S(1)}) custom-call(bf16[512,256]{1,0:T(8,128)(2,1)S(1)} %attend2.1.rest_0_.a0, bf16[512,256]{1,0:T(8,128)(2,1)S(1)} %collective-permute-done.21.a1, bf16[512,256]{1,0:T(8,128)(2,1)S(1)} %collective-permute-done.14.a2, ...), custom_call_target="tpu_custom_call", output_to_operand_aliasing={{0}: (9, {})} | custom-call | tf_op jit(solution)/shard_map/out2/pallas_call | solution.py:420
  97.8 2.3 %collective-permute-done.20.a2 = bf16[768,256]{1,0:T(8,128)(2,1)S(1)} collective-permute-done((bf16[768,256]{1,0:T(8,128)(2,1)S(1)}, bf16[768,256]{1,0:T(8,128)(2,1)S(1)}, u32[]{:S(2)}, u32[]{:S(2)}) %collective-permute-start.20) | collective-permute-done | bytes 393248 | tf_op jit(solution)/shard_map/ppermute | solution.py:265
  100.1 2.1 %collective-permute-start.25 = (bf16[768,256]{1,0:T(8,128)(2,1)S(1)}, bf16[768,256]{1,0:T(8,128)(2,1)S(1)}, u32[]{:S(2)}, u32[]{:S(2)}) collective-permute-start(bf16[768,256]{1,0:T(8,128)(2,1)S(1)} %collective-permute-done.20.a2), channel_id=1, source_target_pairs={{0,1},{1,0},{2,3},{3,2},{4,5},{5,4},{6,7},{7,6},{8,9},{9,8},{10,11... | collective-permute-start | bytes 1179656 | tf_op jit(solution)/shard_map/ppermute | solution.py:265
  102.2 1.3 %collective-permute-done.25.a3 = bf16[768,256]{1,0:T(8,128)(2,1)S(1)} collective-permute-done((bf16[768,256]{1,0:T(8,128)(2,1)S(1)}, bf16[768,256]{1,0:T(8,128)(2,1)S(1)}, u32[]{:S(2)}, u32[]{:S(2)}) %collective-permute-start.25) | collective-permute-done | bytes 393248 | tf_op jit(solution)/shard_map/ppermute | solution.py:265
  103.6 1.9 %out3.1 = (bf16[2048,256]{1,0:T(8,128)(2,1)}, f32[8,128]{1,0:T(8,128)}) custom-call(bf16[768,256]{1,0:T(8,128)(2,1)S(1)} %attend3.1.a0, bf16[768,256]{1,0:T(8,128)(2,1)S(1)} %collective-permute-done.19.a1, bf16[768,256]{1,0:T(8,128)(2,1)S(1)} %collective-permute-done.20.a2, ...), custom_call_target="tpu_custom_call", output_to_operand_aliasing={{0}: (9, {})} | custom-call | tf_op jit(solution)/shard_map/out3/pallas_call | solution.py:420
  (45 shorter events, 0.1 us)
Async XLA Ops:
  0.0 7.2 %copy-start.9 = (bf16[1024,256]{1,0:T(8,128)(2,1)S(1)}, bf16[1024,256]{1,0:T(8,128)(2,1)}, u32[]{:S(2)}) copy-start(bf16[1024,256]{1,0:T(8,128)(2,1)} %wv_hbm.1) | copy-start | bytes 1572868
  0.0 7.2 %copy-start.10 = (bf16[1024,256]{1,0:T(8,128)(2,1)S(1)}, bf16[1024,256]{1,0:T(8,128)(2,1)}, u32[]{:S(2)}) copy-start(bf16[1024,256]{1,0:T(8,128)(2,1)} %wq_hbm.1) | copy-start | bytes 1572868
  0.0 7.2 %copy-start.8 = (bf16[1024,256]{1,0:T(8,128)(2,1)S(1)}, bf16[1024,256]{1,0:T(8,128)(2,1)}, u32[]{:S(2)}) copy-start(bf16[1024,256]{1,0:T(8,128)(2,1)} %wk_hbm.1) | copy-start | bytes 1572868
  4.2 15.9 %collective-permute-start.1 = (bf16[1024,256]{1,0:T(8,128)(2,1)}, bf16[1024,256]{1,0:T(8,128)(2,1)S(1)}, u32[]{:S(2)}, u32[]{:S(2)}) collective-permute-start(bf16[1024,256]{1,0:T(8,128)(2,1)} %get-tuple-element.42.a0), channel_id=1, source_target_pairs={{0,2},{1,3},{2,0},{3,1},{4,6},{5,7},{6,4},{7,5},{8,10},{9,11},{10,... | collective-permute-start | bytes 1572872 | tf_op jit(solution)/shard_map/ppermute | solution.py:265
  5.5 7.9 %copy-start.1 = (bf16[1024,256]{1,0:T(8,128)(2,1)S(1)}, bf16[1024,256]{1,0:T(8,128)(2,1)}, u32[]{:S(2)}) copy-start(bf16[1024,256]{1,0:T(8,128)(2,1)} %get-tuple-element.42.a0) | copy-start | bytes 1572868
  5.5 16.2 %copy-start.16 = (f32[2,27,64]{2,0,1:T(2,128)S(1)}, f32[2,27,64]{2,0,1:T(2,128)}, u32[]{:S(2)}) copy-start(f32[2,27,64]{2,0,1:T(2,128)} %param.12) | copy-start | bytes 41476
  5.5 7.6 %collective-permute-start.2 = (bf16[128,256]{1,0:T(8,128)(2,1)}, bf16[128,256]{1,0:T(8,128)(2,1)S(1)}, u32[]{:S(2)}, u32[]{:S(2)}) collective-permute-start(bf16[128,256]{1,0:T(8,128)(2,1)} %get-tuple-element.43), channel_id=1, source_target_pairs={{0,4},{4,8},{8,12},{12,16},{16,20},{20,24},{24,28},{28,32},{32,36}... | collective-permute-start | bytes 196616 | tf_op jit(solution)/shard_map/ppermute | solution.py:312
  8.1 0.8 copy-start.4
  13.2 10.0 %copy-start.11 = (bf16[128,256]{1,0:T(8,128)(2,1)}, bf16[128,256]{1,0:T(8,128)(2,1)S(1)}, u32[]{:S(2)}) copy-start(bf16[128,256]{1,0:T(8,128)(2,1)S(1)} %collective-permute-done.2.l0) | copy-start | bytes 196612
  13.2 7.0 %collective-permute-start.3 = (bf16[128,256]{1,0:T(8,128)(2,1)S(1)}, bf16[128,256]{1,0:T(8,128)(2,1)S(1)}, u32[]{:S(2)}, u32[]{:S(2)}) collective-permute-start(bf16[128,256]{1,0:T(8,128)(2,1)S(1)} %collective-permute-done.2.l0), channel_id=1, source_target_pairs={{0,2},{1,3},{2,0},{3,1},{4,6},{5,7},{6,4},{7,5},{8,10},{9,11},{10,... | collective-permute-start | bytes 196616 | tf_op jit(solution)/shard_map/ppermute | solution.py:265
  13.4 11.1 %collective-permute-start = (bf16[1024,256]{1,0:T(8,128)(2,1)S(1)}, bf16[1024,256]{1,0:T(8,128)(2,1)S(1)}, u32[]{:S(2)}, u32[]{:S(2)}) collective-permute-start(bf16[1024,256]{1,0:T(8,128)(2,1)S(1)} %copy-done.1), channel_id=1, source_target_pairs={{0,1},{1,0},{2,3},{3,2},{4,5},{5,4},{6,7},{7,6},{8,9},{9,8},{10,11... | collective-permute-start | bytes 1572872 | tf_op jit(solution)/shard_map/ppermute | solution.py:265
  20.1 3.1 %copy-start.13 = (bf16[128,256]{1,0:T(8,128)(2,1)}, bf16[128,256]{1,0:T(8,128)(2,1)S(1)}, u32[]{:S(2)}) copy-start(bf16[128,256]{1,0:T(8,128)(2,1)S(1)} %collective-permute-done.3.l2) | copy-start | bytes 196612
  20.1 4.5 %collective-permute-start.4 = (bf16[1024,256]{1,0:T(8,128)(2,1)S(1)}, bf16[1024,256]{1,0:T(8,128)(2,1)S(1)}, u32[]{:S(2)}, u32[]{:S(2)}) collective-permute-start(bf16[1024,256]{1,0:T(8,128)(2,1)S(1)} %collective-permute-done.1.a2), channel_id=1, source_target_pairs={{0,1},{1,0},{2,3},{3,2},{4,5},{5,4},{6,7},{7,6},{8,9},{9,8},{10,11... | collective-permute-start | bytes 1572872 | tf_op jit(solution)/shard_map/ppermute | solution.py:265
  22.5 2.1 %copy-start.15 = (bf16[144,128]{1,0:T(8,128)(2,1)S(1)}, bf16[144,128]{1,0:T(8,128)(2,1)}, u32[]{:S(2)}) copy-start(bf16[144,128]{1,0:T(8,128)(2,1)} %constant.2.clone.spread_ref) | copy-start | bytes 110596
  23.2 1.3 %collective-permute-start.6 = (bf16[128,256]{1,0:T(8,128)(2,1)S(1)}, bf16[128,256]{1,0:T(8,128)(2,1)S(1)}, u32[]{:S(2)}, u32[]{:S(2)}) collective-permute-start(bf16[128,256]{1,0:T(8,128)(2,1)S(1)} %collective-permute-done.2.l0), channel_id=1, source_target_pairs={{0,1},{1,0},{2,3},{3,2},{4,5},{5,4},{6,7},{7,6},{8,9},{9,8},{10,11... | collective-permute-start | bytes 196616 | tf_op jit(solution)/shard_map/ppermute | solution.py:265
  23.2 1.4 %copy-start.12 = (bf16[128,256]{1,0:T(8,128)(2,1)S(1)}, bf16[128,256]{1,0:T(8,128)(2,1)}, u32[]{:S(2)}) copy-start(bf16[128,256]{1,0:T(8,128)(2,1)} %copy-done.11) | copy-start | bytes 196612
  23.2 1.4 %collective-permute-start.7 = (bf16[128,256]{1,0:T(8,128)(2,1)S(1)}, bf16[128,256]{1,0:T(8,128)(2,1)S(1)}, u32[]{:S(2)}, u32[]{:S(2)}) collective-permute-start(bf16[128,256]{1,0:T(8,128)(2,1)S(1)} %collective-permute-done.3.l2), channel_id=1, source_target_pairs={{0,1},{1,0},{2,3},{3,2},{4,5},{5,4},{6,7},{7,6},{8,9},{9,8},{10,11... | collective-permute-start | bytes 196616 | tf_op jit(solution)/shard_map/ppermute | solution.py:265
  23.7 0.9 copy-start.14
  24.6 4.3 %copy-start.2 = (bf16[1024,256]{1,0:T(8,128)(2,1)}, bf16[1024,256]{1,0:T(8,128)(2,1)S(1)}, u32[]{:S(2)}) copy-start(bf16[1024,256]{1,0:T(8,128)(2,1)S(1)} %collective-permute-done.4.a3) | copy-start | bytes 1572868
  28.9 24.7 %all-to-all-start = ((bf16[8,64,512]{2,1,0:T(8,128)(2,1)}), bf16[8,64,512]{2,1,0:T(8,128)(2,1)S(1)}, u32[]{:S(2)}, u32[]{:S(2)}) async-start(bf16[8,64,512]{2,1,0:T(8,128)(2,1)} %pool.1), calls=%async_computation | async-start | bytes 1048576 | tf_op jit(solution)/shard_map/all_to_all | solution.py:336
  35.7 20.5 %collective-permute-start.5 = (bf16[1536,256]{1,0:T(8,128)(2,1)}, bf16[1536,256]{1,0:T(8,128)(2,1)S(1)}, u32[]{:S(2)}, u32[]{:S(2)}) collective-permute-start(bf16[1536,256]{1,0:T(8,128)(2,1)} %get-tuple-element.50.b0), channel_id=1, source_target_pairs={{0,2},{1,3},{2,0},{3,1},{4,6},{5,7},{6,4},{7,5},{8,10},{9,11},{10,... | collective-permute-start | bytes 2359304 | tf_op jit(solution)/shard_map/ppermute | solution.py:265
  36.9 22.2 %collective-permute-start.8 = (bf16[1280,256]{1,0:T(8,128)(2,1)}, bf16[1280,256]{1,0:T(8,128)(2,1)S(1)}, u32[]{:S(2)}, u32[]{:S(2)}) collective-permute-start(bf16[1280,256]{1,0:T(8,128)(2,1)} %get-tuple-element.54), channel_id=1, source_target_pairs={{0,1},{1,0},{2,3},{3,2},{4,5},{5,4},{6,7},{7,6},{8,9},{9,8},{10,11... | collective-permute-start | bytes 1966088 | tf_op jit(solution)/shard_map/ppermute | solution.py:265
  53.7 2.5 %copy-start.3 = (bf16[1024,256]{1,0:T(8,128)(2,1)S(1)}, bf16[1024,256]{1,0:T(8,128)(2,1)}, u32[]{:S(2)}) copy-start(bf16[1024,256]{1,0:T(8,128)(2,1)} %copy-done.2) | copy-start | bytes 1572868
  53.7 10.5 %collective-permute-start.11 = (bf16[384,512]{1,0:T(8,128)(2,1)S(1)}, bf16[384,512]{1,0:T(8,128)(2,1)S(1)}, u32[]{:S(2)}, u32[]{:S(2)}) collective-permute-start(bf16[384,512]{1,0:T(8,128)(2,1)S(1)} %get-tuple-element.58), channel_id=1, source_target_pairs={{0,32},{4,36},{8,40},{12,44},{16,48},{20,52},{24,56},{28,60},{32,6... | collective-permute-start | bytes 1179656 | tf_op jit(solution)/shard_map/ppermute | solution.py:347
  56.2 13.5 %collective-permute-start.12 = (bf16[384,512]{1,0:T(8,128)(2,1)S(1)}, bf16[384,512]{1,0:T(8,128)(2,1)S(1)}, u32[]{:S(2)}, u32[]{:S(2)}) collective-permute-start(bf16[384,512]{1,0:T(8,128)(2,1)S(1)} %get-tuple-element.59), channel_id=1, source_target_pairs={{32,0},{36,4},{40,8},{44,12},{48,16},{52,20},{56,24},{60,28},{64,3... | collective-permute-start | bytes 1179656 | tf_op jit(solution)/shard_map/ppermute | solution.py:348
  56.2 1.0 copy-start.5
  57.3 3.1 %copy-start.7 = (bf16[1536,256]{1,0:T(8,128)(2,1)S(1)}, bf16[1536,256]{1,0:T(8,128)(2,1)}, u32[]{:S(2)}) copy-start(bf16[1536,256]{1,0:T(8,128)(2,1)} %get-tuple-element.50.b0) | copy-start | bytes 2359300
  58.0 2.0 %collective-permute-start.10 = (bf16[512,256]{1,0:T(8,128)(2,1)S(1)}, bf16[512,256]{1,0:T(8,128)(2,1)S(1)}, u32[]{:S(2)}, u32[]{:S(2)}) collective-permute-start(bf16[512,256]{1,0:T(8,128)(2,1)S(1)} %get-tuple-element.56), channel_id=1, source_target_pairs={{0,1},{1,0},{2,3},{3,2},{4,5},{5,4},{6,7},{7,6},{8,9},{9,8},{10,11... | collective-permute-start | bytes 786440 | tf_op jit(solution)/shard_map/ppermute | solution.py:265
  58.8 1.5 %collective-permute-start.9 = (bf16[512,256]{1,0:T(8,128)(2,1)S(1)}, bf16[512,256]{1,0:T(8,128)(2,1)S(1)}, u32[]{:S(2)}, u32[]{:S(2)}) collective-permute-start(bf16[512,256]{1,0:T(8,128)(2,1)S(1)} %get-tuple-element.55), channel_id=1, source_target_pairs={{0,1},{1,0},{2,3},{3,2},{4,5},{5,4},{6,7},{7,6},{8,9},{9,8},{10,11... | collective-permute-start | bytes 786440 | tf_op jit(solution)/shard_map/ppermute | solution.py:265
  71.9 7.4 %collective-permute-start.13 = (bf16[256,256]{1,0:T(8,128)(2,1)S(1)}, bf16[256,256]{1,0:T(8,128)(2,1)S(1)}, u32[]{:S(2)}, u32[]{:S(2)}) collective-permute-start(bf16[256,256]{1,0:T(8,128)(2,1)S(1)} %attend0.1.rest_0_.a0), channel_id=1, source_target_pairs={{0,2},{1,3},{2,0},{3,1},{4,6},{5,7},{6,4},{7,5},{8,10},{9,11},{10,... | collective-permute-start | bytes 393224 | tf_op jit(solution)/shard_map/ppermute | solution.py:265
  72.3 11.4 %collective-permute-start.18 = (bf16[512,256]{1,0:T(8,128)(2,1)S(1)}, bf16[512,256]{1,0:T(8,128)(2,1)S(1)}, u32[]{:S(2)}, u32[]{:S(2)}) collective-permute-start(bf16[512,256]{1,0:T(8,128)(2,1)S(1)} %get-tuple-element.65), channel_id=1, source_target_pairs={{0,1},{1,0},{2,3},{3,2},{4,5},{5,4},{6,7},{7,6},{8,9},{9,8},{10,11... | collective-permute-start | bytes 786440 | tf_op jit(solution)/shard_map/ppermute | solution.py:265
  77.8 8.0 %collective-permute-start.15 = (bf16[512,256]{1,0:T(8,128)(2,1)S(1)}, bf16[512,256]{1,0:T(8,128)(2,1)S(1)}, u32[]{:S(2)}, u32[]{:S(2)}) collective-permute-start(bf16[512,256]{1,0:T(8,128)(2,1)S(1)} %attend1.1.rest_0_.a0), channel_id=1, source_target_pairs={{0,2},{1,3},{2,0},{3,1},{4,6},{5,7},{6,4},{7,5},{8,10},{9,11},{10,... | collective-permute-start | bytes 786440 | tf_op jit(solution)/shard_map/ppermute | solution.py:265
  79.0 4.7 %collective-permute-start.16 = (bf16[256,256]{1,0:T(8,128)(2,1)S(1)}, bf16[256,256]{1,0:T(8,128)(2,1)S(1)}, u32[]{:S(2)}, u32[]{:S(2)}) collective-permute-start(bf16[256,256]{1,0:T(8,128)(2,1)S(1)} %attend0.1.rest_0_.a0), channel_id=1, source_target_pairs={{0,1},{1,0},{2,3},{3,2},{4,5},{5,4},{6,7},{7,6},{8,9},{9,8},{10,11... | collective-permute-start | bytes 393224 | tf_op jit(solution)/shard_map/ppermute | solution.py:265
  79.3 5.4 %copy-start = (bf16[2048,256]{1,0:T(8,128)(2,1)S(1)}, bf16[2048,256]{1,0:T(8,128)(2,1)}, u32[]{:S(2)}) copy-start(bf16[2048,256]{1,0:T(8,128)(2,1)} %tokens_ref.7) | copy-start | bytes 3145732
  79.3 5.4 %copy-start.6 = (bf16[256,256]{1,0:T(8,128)(2,1)S(1)}, bf16[256,256]{1,0:T(8,128)(2,1)}, u32[]{:S(2)}) copy-start(bf16[256,256]{1,0:T(8,128)(2,1)} %get-tuple-element.64.w0) | copy-start | bytes 393220
  82.8 11.0 %collective-permute-start.14 = (bf16[512,256]{1,0:T(8,128)(2,1)S(1)}, bf16[512,256]{1,0:T(8,128)(2,1)S(1)}, u32[]{:S(2)}, u32[]{:S(2)}) collective-permute-start(bf16[512,256]{1,0:T(8,128)(2,1)S(1)} %attend2.1.rest_0_.a0), channel_id=1, source_target_pairs={{0,2},{1,3},{2,0},{3,1},{4,6},{5,7},{6,4},{7,5},{8,10},{9,11},{10,... | collective-permute-start | bytes 786440 | tf_op jit(solution)/shard_map/ppermute | solution.py:265
  83.2 1.5 %collective-permute-start.17 = (bf16[256,256]{1,0:T(8,128)(2,1)S(1)}, bf16[256,256]{1,0:T(8,128)(2,1)S(1)}, u32[]{:S(2)}, u32[]{:S(2)}) collective-permute-start(bf16[256,256]{1,0:T(8,128)(2,1)S(1)} %collective-permute-done.13.rest_1_.a2), channel_id=1, source_target_pairs={{0,1},{1,0},{2,3},{3,2},{4,5},{5,4},{6,7},{7,6},{8,9},{9,8},{10,11... | collective-permute-start | bytes 393224 | tf_op jit(solution)/shard_map/ppermute | solution.py:265
  90.6 9.5 %collective-permute-start.20 = (bf16[768,256]{1,0:T(8,128)(2,1)S(1)}, bf16[768,256]{1,0:T(8,128)(2,1)S(1)}, u32[]{:S(2)}, u32[]{:S(2)}) collective-permute-start(bf16[768,256]{1,0:T(8,128)(2,1)S(1)} %attend3.1.a0), channel_id=1, source_target_pairs={{0,2},{1,3},{2,0},{3,1},{4,6},{5,7},{6,4},{7,5},{8,10},{9,11},{10,... | collective-permute-start | bytes 1179656 | tf_op jit(solution)/shard_map/ppermute | solution.py:265
  91.8 2.6 %collective-permute-start.23 = (bf16[512,256]{1,0:T(8,128)(2,1)S(1)}, bf16[512,256]{1,0:T(8,128)(2,1)S(1)}, u32[]{:S(2)}, u32[]{:S(2)}) collective-permute-start(bf16[512,256]{1,0:T(8,128)(2,1)S(1)} %attend1.1.rest_0_.a0), channel_id=1, source_target_pairs={{0,1},{1,0},{2,3},{3,2},{4,5},{5,4},{6,7},{7,6},{8,9},{9,8},{10,11... | collective-permute-start | bytes 786440 | tf_op jit(solution)/shard_map/ppermute | solution.py:265
  93.3 3.2 %collective-permute-start.21 = (bf16[512,256]{1,0:T(8,128)(2,1)S(1)}, bf16[512,256]{1,0:T(8,128)(2,1)S(1)}, u32[]{:S(2)}, u32[]{:S(2)}) collective-permute-start(bf16[512,256]{1,0:T(8,128)(2,1)S(1)} %attend2.1.rest_0_.a0), channel_id=1, source_target_pairs={{0,1},{1,0},{2,3},{3,2},{4,5},{5,4},{6,7},{7,6},{8,9},{9,8},{10,11... | collective-permute-start | bytes 786440 | tf_op jit(solution)/shard_map/ppermute | solution.py:265
  93.3 1.9 %collective-permute-start.24 = (bf16[512,256]{1,0:T(8,128)(2,1)S(1)}, bf16[512,256]{1,0:T(8,128)(2,1)S(1)}, u32[]{:S(2)}, u32[]{:S(2)}) collective-permute-start(bf16[512,256]{1,0:T(8,128)(2,1)S(1)} %collective-permute-done.15.rest_2_.a2), channel_id=1, source_target_pairs={{0,1},{1,0},{2,3},{3,2},{4,5},{5,4},{6,7},{7,6},{8,9},{9,8},{10,11... | collective-permute-start | bytes 786440 | tf_op jit(solution)/shard_map/ppermute | solution.py:265
  93.8 2.7 %collective-permute-start.22 = (bf16[512,256]{1,0:T(8,128)(2,1)S(1)}, bf16[512,256]{1,0:T(8,128)(2,1)S(1)}, u32[]{:S(2)}, u32[]{:S(2)}) collective-permute-start(bf16[512,256]{1,0:T(8,128)(2,1)S(1)} %collective-permute-done.14.a2), channel_id=1, source_target_pairs={{0,1},{1,0},{2,3},{3,2},{4,5},{5,4},{6,7},{7,6},{8,9},{9,8},{10,11... | collective-permute-start | bytes 786440 | tf_op jit(solution)/shard_map/ppermute | solution.py:265
  94.5 7.8 %collective-permute-start.19 = (bf16[768,256]{1,0:T(8,128)(2,1)S(1)}, bf16[768,256]{1,0:T(8,128)(2,1)S(1)}, u32[]{:S(2)}, u32[]{:S(2)}) collective-permute-start(bf16[768,256]{1,0:T(8,128)(2,1)S(1)} %attend3.1.a0), channel_id=1, source_target_pairs={{0,1},{1,0},{2,3},{3,2},{4,5},{5,4},{6,7},{7,6},{8,9},{9,8},{10,11... | collective-permute-start | bytes 1179656 | tf_op jit(solution)/shard_map/ppermute | solution.py:265
  100.1 3.4 %collective-permute-start.25 = (bf16[768,256]{1,0:T(8,128)(2,1)S(1)}, bf16[768,256]{1,0:T(8,128)(2,1)S(1)}, u32[]{:S(2)}, u32[]{:S(2)}) collective-permute-start(bf16[768,256]{1,0:T(8,128)(2,1)S(1)} %collective-permute-done.20.a2), channel_id=1, source_target_pairs={{0,1},{1,0},{2,3},{3,2},{4,5},{5,4},{6,7},{7,6},{8,9},{9,8},{10,11... | collective-permute-start | bytes 1179656 | tf_op jit(solution)/shard_map/ppermute | solution.py:265

commit v2 on v1

--- a/solution.py
+++ b/solution.py
@@ -54,9 +54,8 @@
 
 
 def move_matrix(back):
-    shape = (FRAME, FRAME)
-    token = lax.broadcasted_iota(jnp.int32, shape, 0 if back else 1)
-    place = lax.broadcasted_iota(jnp.int32, shape, 1 if back else 0)
+    token = lax.broadcasted_iota(jnp.int32, (FRAME, 1) if back else (1, FRAME), 0 if back else 1)
+    place = lax.broadcasted_iota(jnp.int32, (FRAME, FRAME), 1 if back else 0)
     return jnp.where(place_of(token) == place, 1.0, 0.0).astype(jnp.bfloat16)
 
 
@@ -113,7 +112,7 @@
     across_ref[count + width :, :] = columns(3)
 
 
-def pack_kernel(wk_hbm, wv_hbm, wq_hbm, key_value_ref, query_ref, sems):
+def pack_kernel(wk_hbm, wv_hbm, wq_hbm, pool_ref, key_value_ref, query_ref, taps_ref, sems):
     me = lax.axis_index("chan")
     width = query_ref.shape[1]
     copies = []
@@ -131,6 +130,8 @@
         ]
     for copy in copies:
         copy.start()
+    heads = width // HDIM
+    taps_ref[...] = jnp.concatenate([pool_ref[0]] * heads + [pool_ref[1]] * heads, axis=1)
     for copy in copies:
         copy.wait()
 
@@ -271,9 +272,6 @@
     devices = lax.axis_size("tm")
     bf16 = jnp.bfloat16
     tap_gather = jnp.asarray(TAP_GATHER)
-    taps = jnp.concatenate(
-        [jnp.tile(pool_kernel[0], (1, width // HDIM)), jnp.tile(pool_kernel[1], (1, width // HDIM))], axis=1
-    )
     anywhere = pl.BlockSpec(memory_space=pl.ANY)
 
     hbm = pl.BlockSpec(memory_space=pltpu.HBM)
@@ -299,16 +297,20 @@
         cost_estimate=cost(2 * rows * FRAME * width, 4 * rows * width),
         name="arrange",
     )(tokens, w_out)
-    key_value_weights, query_weights = pl.pallas_call(
+    key_value_weights, query_weights, taps = pl.pallas_call(
         pack_kernel,
-        out_shape=(jax.ShapeDtypeStruct((D, 2 * width), bf16), jax.ShapeDtypeStruct((D, width), bf16)),
-        in_specs=[hbm] * 3,
-        out_specs=tuple(vmem(2)),
+        out_shape=(
+            jax.ShapeDtypeStruct((D, 2 * width), bf16),
+            jax.ShapeDtypeStruct((D, width), bf16),
+            jax.ShapeDtypeStruct((pool_kernel.shape[1], 2 * width), jnp.float32),
+        ),
+        in_specs=[hbm] * 3 + vmem(1),
+        out_specs=tuple(vmem(3)),
         scratch_shapes=[pltpu.SemaphoreType.DMA((12,))],
         compiler_params=params(8),
         cost_estimate=cost(0, 12 * D * width),
         name="pack",
-    )(w_key, w_value, w_query)
+    )(w_key, w_value, w_query, pool_kernel)
     last = lax.ppermute(last, "tm", [(i, (i + 1) % devices) for i in range(devices)])
 
     last, key_value_weights = lax.optimization_barrier((last, key_value_weights))

time: 106 us -> 105 us (level)
    another operation x5 -> x0, local copies, waits for them, and re-layouts: 1.42 us -> none  [the longest x3 0.71 us: per_device(): jnp.tile(pool_kernel[1], (1, width // HDIM))]
    ppermute x23, waiting for transfers between devices: 11.8 us -> 12.9 us  [swap(): return lax.ppermute(array, 'chan', [(i, i ^ k) for i in range(4)])]
    unnamed x34 -> x27, local copies, waits for them, and re-layouts: 1.9 us -> 2.67 us
  transfers between devices with their start and end apart: 27 -> 27, of which waited for: 14 -> 15; matrix products, arithmetic and copies ran while one was open for 2% -> 0% of each run, Pallas kernels for 19% -> 19%
where the time goes in v2:
time: 105 us
  waiting for transfers between devices  39.4 us (38%)
  Pallas kernels  32.5 us (31%)
  starting transfers between devices  30.4 us (29%)
  local copies, waits for them, and re-layouts  2.67 us (3%)
    ppermute x23, starting transfers between devices, swap(): return lax.ppermute(array, 'chan', [(i, i ^ k) for i in range(4)])  19.5 us
    all_to_all x1, waiting for transfers between devices, per_device(): lax.all_to_all(block, 'tm', 0, 0, axis_index_groups=rings)  15.8 us
    pallas_call x4, Pallas kernels, attend(): pl.pallas_call(attend_kernel, out_shape=jax.ShapeDtypeStruct((chunk, widt...  14 us
    ppermute x23, waiting for transfers between devices, swap(): return lax.ppermute(array, 'chan', [(i, i ^ k) for i in range(4)])  12.9 us
    all_to_all x1, starting transfers between devices, per_device(): lax.all_to_all(block, 'tm', 0, 0, axis_index_groups=rings)  6.79 us
    ppermute x1, waiting for transfers between devices, per_device(): lax.ppermute(head, 'tm', [((i + RING) % devices, i) for i in range(device...  5.49 us
    pallas_call x4, Pallas kernels, finish(): pl.pallas_call(out_kernel, grid=(tiles,), out_shape=(jax.ShapeDtypeStruct...  5.47 us
    pallas_call x1, Pallas kernels, per_device(): pl.pallas_call(pool_kernel_body, out_shape=jax.ShapeDtypeStruct((RING, fr...  4.3 us
  transfers between devices with their start and end apart: 27, of which 15 were waited for; matrix products, arithmetic and copies ran while one was open for 0% of the time, Pallas kernels for 19%

profile of v2, /device:TPU:25, one launch (start us, length us, event | category | flops | bytes accessed | tf_op | source)
XLA Modules:
  0.0 105.1 jit_solution(3406839065025376869)
XLA Ops:
  0.0 4.2 %arrange.1 = (bf16[1024,256]{1,0:T(8,128)(2,1)}, bf16[128,256]{1,0:T(8,128)(2,1)}, bf16[1536,256]{1,0:T(8,128)(2,1)}, bf16[1280,256]{1,0:T(8,128)(2,1)}, bf16[256,256]{1,0:T(8,128)(2,1)}) custom-call(bf16[2048,256]{1,0:T(8,128)(2,1)} %tokens_ref.7, bf16[256,1024]{1,0:T(8,128)(2,1)} %w_out_hbm.1), custom_call_target="tpu_custom_call" | custom-call | flops 268435456 | bytes 2097152 | tf_op jit(solution)/shard_map/arrange/pallas_call | solution.py:279
  4.3 1.3 %collective-permute-start.1 = (bf16[1024,256]{1,0:T(8,128)(2,1)}, bf16[1024,256]{1,0:T(8,128)(2,1)S(1)}, u32[]{:S(2)}, u32[]{:S(2)}) collective-permute-start(bf16[1024,256]{1,0:T(8,128)(2,1)} %get-tuple-element.43.a0), channel_id=1, source_target_pairs={{0,2},{1,3},{2,0},{3,1},{4,6},{5,7},{6,4},{7,5},{8,10},{9,11},{10,... | collective-permute-start | bytes 1572872 | tf_op jit(solution)/shard_map/ppermute | solution.py:266
  5.6 1.6 %collective-permute-start.2 = (bf16[128,256]{1,0:T(8,128)(2,1)}, bf16[128,256]{1,0:T(8,128)(2,1)S(1)}, u32[]{:S(2)}, u32[]{:S(2)}) collective-permute-start(bf16[128,256]{1,0:T(8,128)(2,1)} %get-tuple-element.44), channel_id=1, source_target_pairs={{0,4},{4,8},{8,12},{12,16},{16,20},{20,24},{24,28},{28,32},{32,36}... | collective-permute-start | bytes 196616 | tf_op jit(solution)/shard_map/ppermute | solution.py:314
  7.2 0.0 copy-start.11
  7.2 1.0 pack.1
  8.3 0.8 copy-done.4
  9.0 4.1 %collective-permute-done.2.l0 = bf16[128,256]{1,0:T(8,128)(2,1)S(1)} collective-permute-done((bf16[128,256]{1,0:T(8,128)(2,1)}, bf16[128,256]{1,0:T(8,128)(2,1)S(1)}, u32[]{:S(2)}, u32[]{:S(2)}) %collective-permute-start.2) | collective-permute-done | bytes 65568 | tf_op jit(solution)/shard_map/ppermute | solution.py:314
  13.2 0.3 collective-permute-start.3
  13.4 2.1 %collective-permute-start = (bf16[1024,256]{1,0:T(8,128)(2,1)S(1)}, bf16[1024,256]{1,0:T(8,128)(2,1)S(1)}, u32[]{:S(2)}, u32[]{:S(2)}) collective-permute-start(bf16[1024,256]{1,0:T(8,128)(2,1)S(1)} %copy-done.1), channel_id=1, source_target_pairs={{0,1},{1,0},{2,3},{3,2},{4,5},{5,4},{6,7},{7,6},{8,9},{9,8},{10,11... | collective-permute-start | bytes 1572872 | tf_op jit(solution)/shard_map/ppermute | solution.py:266
  15.5 4.6 %collective-permute-done.3.l2 = bf16[128,256]{1,0:T(8,128)(2,1)S(1)} collective-permute-done((bf16[128,256]{1,0:T(8,128)(2,1)S(1)}, bf16[128,256]{1,0:T(8,128)(2,1)S(1)}, u32[]{:S(2)}, u32[]{:S(2)}) %collective-permute-start.3) | collective-permute-done | bytes 65568 | tf_op jit(solution)/shard_map/ppermute | solution.py:266
  20.2 0.0 collective-permute-done.1.a2
  20.2 1.5 %collective-permute-start.4 = (bf16[1024,256]{1,0:T(8,128)(2,1)S(1)}, bf16[1024,256]{1,0:T(8,128)(2,1)S(1)}, u32[]{:S(2)}, u32[]{:S(2)}) collective-permute-start(bf16[1024,256]{1,0:T(8,128)(2,1)S(1)} %collective-permute-done.1.a2), channel_id=1, source_target_pairs={{0,1},{1,0},{2,3},{3,2},{4,5},{5,4},{6,7},{7,6},{8,9},{9,8},{10,11... | collective-permute-start | bytes 1572872 | tf_op jit(solution)/shard_map/ppermute | solution.py:266
  21.7 0.0 collective-permute-start.6
  21.7 0.5 collective-permute-start.7
  22.2 1.1 %collective-permute-done.6.l1 = bf16[128,256]{1,0:T(8,128)(2,1)S(1)} collective-permute-done((bf16[128,256]{1,0:T(8,128)(2,1)S(1)}, bf16[128,256]{1,0:T(8,128)(2,1)S(1)}, u32[]{:S(2)}, u32[]{:S(2)}) %collective-permute-start.6) | collective-permute-done | bytes 65568 | tf_op jit(solution)/shard_map/ppermute | solution.py:266
  23.3 0.1 collective-permute-done.7.l3
  23.4 4.3 %pool.1 = bf16[8,64,512]{2,1,0:T(8,128)(2,1)} custom-call(bf16[1024,256]{1,0:T(8,128)(2,1)S(1)} %copy-done.1, bf16[1024,256]{1,0:T(8,128)(2,1)S(1)} %collective-permute-done.a1, bf16[1024,256]{1,0:T(8,128)(2,1)S(1)} %collective-permute-done.1.a2, bf16[1024,256]{1,0:T(8,128)(2,1)S(1)} %collective-permute-done.4.a3, ...), custom_call_target="tpu_custom_call" | custom-call | flops 1073741824 | bytes 4194304 | tf_op jit(solution)/shard_map/pool/pallas_call | solution.py:326
  27.7 0.8 copy-done.2
  28.5 6.8 %all-to-all-start = ((bf16[8,64,512]{2,1,0:T(8,128)(2,1)}), bf16[8,64,512]{2,1,0:T(8,128)(2,1)S(1)}, u32[]{:S(2)}, u32[]{:S(2)}) async-start(bf16[8,64,512]{2,1,0:T(8,128)(2,1)} %pool.1), calls=%async_computation | async-start | bytes 1048576 | tf_op jit(solution)/shard_map/all_to_all | solution.py:338
  35.3 1.2 %collective-permute-start.5 = (bf16[1536,256]{1,0:T(8,128)(2,1)}, bf16[1536,256]{1,0:T(8,128)(2,1)S(1)}, u32[]{:S(2)}, u32[]{:S(2)}) collective-permute-start(bf16[1536,256]{1,0:T(8,128)(2,1)} %get-tuple-element.51.b0), channel_id=1, source_target_pairs={{0,2},{1,3},{2,0},{3,1},{4,6},{5,7},{6,4},{7,5},{8,10},{9,11},{10,... | collective-permute-start | bytes 2359304 | tf_op jit(solution)/shard_map/ppermute | solution.py:266
  36.5 0.9 collective-permute-start.8
  37.5 15.8 %all-to-all-done = bf16[8,64,512]{2,1,0:T(8,128)(2,1)S(1)} async-done(((bf16[8,64,512]{2,1,0:T(8,128)(2,1)}), bf16[8,64,512]{2,1,0:T(8,128)(2,1)S(1)}, u32[]{:S(2)}, u32[]{:S(2)}) %all-to-all-start) | async-done | bytes 524320 | tf_op jit(solution)/shard_map/all_to_all | solution.py:338
  53.3 0.1 ends.1
  53.3 2.5 %collective-permute-start.11 = (bf16[384,512]{1,0:T(8,128)(2,1)S(1)}, bf16[384,512]{1,0:T(8,128)(2,1)S(1)}, u32[]{:S(2)}, u32[]{:S(2)}) collective-permute-start(bf16[384,512]{1,0:T(8,128)(2,1)S(1)} %get-tuple-element.60), channel_id=1, source_target_pairs={{0,32},{4,36},{8,40},{12,44},{16,48},{20,52},{24,56},{28,60},{32,6... | collective-permute-start | bytes 1179656 | tf_op jit(solution)/shard_map/ppermute | solution.py:349
  55.9 1.0 copy-done.5
  56.9 0.7 tap_query.1
  57.6 0.9 collective-permute-start.10
  58.5 0.3 collective-permute-start.9
  58.7 0.0 collective-permute-done.8.b1.w1
  58.7 0.9 collective-permute-done.10.c1
  59.6 0.4 collective-permute-done.9.c0
  60.0 2.7 %query.1 = (bf16[256,256]{1,0:T(8,128)(2,1)S(1)}, bf16[512,256]{1,0:T(8,128)(2,1)S(1)}, bf16[512,256]{1,0:T(8,128)(2,1)S(1)}, bf16[768,256]{1,0:T(8,128)(2,1)S(1)}) custom-call(bf16[1024,256]{1,0:T(8,128)(2,1)S(1)} %get-tuple-element.55.q_ref, bf16[1536,256]{1,0:T(8,128)(2,1)S(1)} %copy-done.7, bf16[1280,256]{1,0:T(8,128)(2,1)S(1)} %collective-permute-done.8.b1.w1, ...), custom_call_target="tpu_custom_call" | custom-call | tf_op jit(solution)/shard_map/query/pallas_call | solution.py:362
  62.7 1.1 %collective-permute-done.11.before_ref = bf16[384,512]{1,0:T(8,128)(2,1)S(1)} collective-permute-done((bf16[384,512]{1,0:T(8,128)(2,1)S(1)}, bf16[384,512]{1,0:T(8,128)(2,1)S(1)}, u32[]{:S(2)}, u32[]{:S(2)}) %collective-permute-start.11) | collective-permute-done | bytes 393248 | tf_op jit(solution)/shard_map/ppermute | solution.py:349
  63.8 5.5 %collective-permute-done.12.after_ref = bf16[384,512]{1,0:T(8,128)(2,1)S(1)} collective-permute-done((bf16[384,512]{1,0:T(8,128)(2,1)S(1)}, bf16[384,512]{1,0:T(8,128)(2,1)S(1)}, u32[]{:S(2)}, u32[]{:S(2)}) %collective-permute-start.12) | collective-permute-done | bytes 393248 | tf_op jit(solution)/shard_map/ppermute | solution.py:350
  69.3 2.2 %attend0.1.rest_0_.a0 = bf16[256,256]{1,0:T(8,128)(2,1)S(1)} custom-call(bf16[256,256]{1,0:T(8,128)(2,1)S(1)} %get-tuple-element.63.q_ref, bf16[384,512]{1,0:T(8,128)(2,1)S(1)} %collective-permute-done.11.before_ref, bf16[512,512]{1,0:T(8,128)(2,1)S(1)} %bitcast.3, bf16[384,512]{1,0:T(8,128)(2,1)S(1)} %collective-permute-done.12.after_ref), custom_call_target="tpu_custom_call" | custom-call | tf_op jit(solution)/shard_map/attend0/pallas_call | solution.py:393
  71.5 0.4 collective-permute-start.13
  71.9 1.9 %collective-permute-start.18 = (bf16[512,256]{1,0:T(8,128)(2,1)S(1)}, bf16[512,256]{1,0:T(8,128)(2,1)S(1)}, u32[]{:S(2)}, u32[]{:S(2)}) collective-permute-start(bf16[512,256]{1,0:T(8,128)(2,1)S(1)} %get-tuple-element.67), channel_id=1, source_target_pairs={{0,1},{1,0},{2,3},{3,2},{4,5},{5,4},{6,7},{7,6},{8,9},{9,8},{10,11... | collective-permute-start | bytes 786440 | tf_op jit(solution)/shard_map/ppermute | solution.py:266
  73.9 3.5 %attend1.1.rest_0_.a0 = bf16[512,256]{1,0:T(8,128)(2,1)S(1)} custom-call(bf16[512,256]{1,0:T(8,128)(2,1)S(1)} %get-tuple-element.62.q_ref, bf16[384,512]{1,0:T(8,128)(2,1)S(1)} %collective-permute-done.11.before_ref, bf16[512,512]{1,0:T(8,128)(2,1)S(1)} %bitcast.4, bf16[384,512]{1,0:T(8,128)(2,1)S(1)} %collective-permute-done.12.after_ref, ...), custom_call_target="tpu_custom_call" | custom-call | tf_op jit(solution)/shard_map/attend1/pallas_call | solution.py:393
  77.4 1.3 %collective-permute-start.15 = (bf16[512,256]{1,0:T(8,128)(2,1)S(1)}, bf16[512,256]{1,0:T(8,128)(2,1)S(1)}, u32[]{:S(2)}, u32[]{:S(2)}) collective-permute-start(bf16[512,256]{1,0:T(8,128)(2,1)S(1)} %attend1.1.rest_0_.a0), channel_id=1, source_target_pairs={{0,2},{1,3},{2,0},{3,1},{4,6},{5,7},{6,4},{7,5},{8,10},{9,11},{10,... | collective-permute-start | bytes 786440 | tf_op jit(solution)/shard_map/ppermute | solution.py:266
  78.6 0.3 collective-permute-start.16
  78.9 0.0 collective-permute-done.13.rest_1_.a2
  78.9 3.5 %attend2.1.rest_0_.a0 = bf16[512,256]{1,0:T(8,128)(2,1)S(1)} custom-call(bf16[512,256]{1,0:T(8,128)(2,1)S(1)} %get-tuple-element.59.q_ref, bf16[384,512]{1,0:T(8,128)(2,1)S(1)} %collective-permute-done.11.before_ref, bf16[512,512]{1,0:T(8,128)(2,1)S(1)} %bitcast.5, bf16[384,512]{1,0:T(8,128)(2,1)S(1)} %collective-permute-done.12.after_ref, ...), custom_call_target="tpu_custom_call" | custom-call | tf_op jit(solution)/shard_map/attend2/pallas_call | solution.py:393
  82.4 0.4 collective-permute-start.14
  82.8 0.5 collective-permute-start.17
  83.3 0.0 collective-permute-done.18.w3
  83.3 1.0 collective-permute-done.17.a3
  84.3 1.0 out0.1
  85.3 0.1 collective-permute-done.15.rest_2_.a2
  85.4 4.8 %attend3.1.a0 = bf16[768,256]{1,0:T(8,128)(2,1)S(1)} custom-call(bf16[768,256]{1,0:T(8,128)(2,1)S(1)} %get-tuple-element.64.q_ref, bf16[384,512]{1,0:T(8,128)(2,1)S(1)} %collective-permute-done.11.before_ref, bf16[512,512]{1,0:T(8,128)(2,1)S(1)} %bitcast.6, bf16[384,512]{1,0:T(8,128)(2,1)S(1)} %collective-permute-done.12.after_ref, ...), custom_call_target="tpu_custom_call" | custom-call | tf_op jit(solution)/shard_map/attend3/pallas_call | solution.py:393
  90.2 1.3 %collective-permute-start.20 = (bf16[768,256]{1,0:T(8,128)(2,1)S(1)}, bf16[768,256]{1,0:T(8,128)(2,1)S(1)}, u32[]{:S(2)}, u32[]{:S(2)}) collective-permute-start(bf16[768,256]{1,0:T(8,128)(2,1)S(1)} %attend3.1.a0), channel_id=1, source_target_pairs={{0,2},{1,3},{2,0},{3,1},{4,6},{5,7},{6,4},{7,5},{8,10},{9,11},{10,... | collective-permute-start | bytes 1179656 | tf_op jit(solution)/shard_map/ppermute | solution.py:266
  91.5 1.4 %collective-permute-start.23 = (bf16[512,256]{1,0:T(8,128)(2,1)S(1)}, bf16[512,256]{1,0:T(8,128)(2,1)S(1)}, u32[]{:S(2)}, u32[]{:S(2)}) collective-permute-start(bf16[512,256]{1,0:T(8,128)(2,1)S(1)} %attend1.1.rest_0_.a0), channel_id=1, source_target_pairs={{0,1},{1,0},{2,3},{3,2},{4,5},{5,4},{6,7},{7,6},{8,9},{9,8},{10,11... | collective-permute-start | bytes 786440 | tf_op jit(solution)/shard_map/ppermute | solution.py:266
  92.9 0.0 collective-permute-start.21
  92.9 0.5 collective-permute-start.24
  93.4 0.0 collective-permute-start.22
  93.4 0.6 collective-permute-done.23.a1
  94.1 0.4 collective-permute-start.19
  94.4 0.4 collective-permute-done.24.a3
  94.8 1.3 %out1.1 = (bf16[2048,256]{1,0:T(8,128)(2,1)}, f32[8,128]{1,0:T(8,128)}) custom-call(bf16[512,256]{1,0:T(8,128)(2,1)S(1)} %attend1.1.rest_0_.a0, bf16[512,256]{1,0:T(8,128)(2,1)S(1)} %collective-permute-done.23.a1, bf16[512,256]{1,0:T(8,128)(2,1)S(1)} %collective-permute-done.15.rest_2_.a2, ...), custom_call_target="tpu_custom_call", output_to_operand_aliasing={{0}: (9, {})} | custom-call | tf_op jit(solution)/shard_map/out1/pallas_call | solution.py:422
  96.1 1.3 %out2.1 = (bf16[2048,256]{1,0:T(8,128)(2,1)}, f32[8,128]{1,0:T(8,128)S(1)}) custom-call(bf16[512,256]{1,0:T(8,128)(2,1)S(1)} %attend2.1.rest_0_.a0, bf16[512,256]{1,0:T(8,128)(2,1)S(1)} %collective-permute-done.21.a1, bf16[512,256]{1,0:T(8,128)(2,1)S(1)} %collective-permute-done.14.a2, ...), custom_call_target="tpu_custom_call", output_to_operand_aliasing={{0}: (9, {})} | custom-call | tf_op jit(solution)/shard_map/out2/pallas_call | solution.py:422
  97.4 2.3 %collective-permute-done.20.a2 = bf16[768,256]{1,0:T(8,128)(2,1)S(1)} collective-permute-done((bf16[768,256]{1,0:T(8,128)(2,1)S(1)}, bf16[768,256]{1,0:T(8,128)(2,1)S(1)}, u32[]{:S(2)}, u32[]{:S(2)}) %collective-permute-start.20) | collective-permute-done | bytes 393248 | tf_op jit(solution)/shard_map/ppermute | solution.py:266
  99.7 2.1 %collective-permute-start.25 = (bf16[768,256]{1,0:T(8,128)(2,1)S(1)}, bf16[768,256]{1,0:T(8,128)(2,1)S(1)}, u32[]{:S(2)}, u32[]{:S(2)}) collective-permute-start(bf16[768,256]{1,0:T(8,128)(2,1)S(1)} %collective-permute-done.20.a2), channel_id=1, source_target_pairs={{0,1},{1,0},{2,3},{3,2},{4,5},{5,4},{6,7},{7,6},{8,9},{9,8},{10,11... | collective-permute-start | bytes 1179656 | tf_op jit(solution)/shard_map/ppermute | solution.py:266
  101.8 0.0 collective-permute-done.19.a1
  101.8 1.3 %collective-permute-done.25.a3 = bf16[768,256]{1,0:T(8,128)(2,1)S(1)} collective-permute-done((bf16[768,256]{1,0:T(8,128)(2,1)S(1)}, bf16[768,256]{1,0:T(8,128)(2,1)S(1)}, u32[]{:S(2)}, u32[]{:S(2)}) %collective-permute-start.25) | collective-permute-done | bytes 393248 | tf_op jit(solution)/shard_map/ppermute | solution.py:266
  103.2 1.9 %out3.1 = (bf16[2048,256]{1,0:T(8,128)(2,1)}, f32[8,128]{1,0:T(8,128)}) custom-call(bf16[768,256]{1,0:T(8,128)(2,1)S(1)} %attend3.1.a0, bf16[768,256]{1,0:T(8,128)(2,1)S(1)} %collective-permute-done.19.a1, bf16[768,256]{1,0:T(8,128)(2,1)S(1)} %collective-permute-done.20.a2, ...), custom_call_target="tpu_custom_call", output_to_operand_aliasing={{0}: (9, {})} | custom-call | tf_op jit(solution)/shard_map/out3/pallas_call | solution.py:422
  (31 shorter events, 0.1 us)
Async XLA Ops:
  0.0 7.2 %copy-start.12 = (f32[2,27,64]{2,0,1:T(2,128)S(1)}, f32[2,27,64]{2,0,1:T(2,128)}, u32[]{:S(2)}) copy-start(f32[2,27,64]{2,0,1:T(2,128)} %param.12) | copy-start | bytes 41476
  0.0 7.2 %copy-start.9 = (bf16[1024,256]{1,0:T(8,128)(2,1)S(1)}, bf16[1024,256]{1,0:T(8,128)(2,1)}, u32[]{:S(2)}) copy-start(bf16[1024,256]{1,0:T(8,128)(2,1)} %wv_hbm.1) | copy-start | bytes 1572868
  0.0 7.2 %copy-start.10 = (bf16[1024,256]{1,0:T(8,128)(2,1)S(1)}, bf16[1024,256]{1,0:T(8,128)(2,1)}, u32[]{:S(2)}) copy-start(bf16[1024,256]{1,0:T(8,128)(2,1)} %wq_hbm.1) | copy-start | bytes 1572868
  0.0 7.2 %copy-start.8 = (bf16[1024,256]{1,0:T(8,128)(2,1)S(1)}, bf16[1024,256]{1,0:T(8,128)(2,1)}, u32[]{:S(2)}) copy-start(bf16[1024,256]{1,0:T(8,128)(2,1)} %wk_hbm.1) | copy-start | bytes 1572868
  4.3 15.9 %collective-permute-start.1 = (bf16[1024,256]{1,0:T(8,128)(2,1)}, bf16[1024,256]{1,0:T(8,128)(2,1)S(1)}, u32[]{:S(2)}, u32[]{:S(2)}) collective-permute-start(bf16[1024,256]{1,0:T(8,128)(2,1)} %get-tuple-element.43.a0), channel_id=1, source_target_pairs={{0,2},{1,3},{2,0},{3,1},{4,6},{5,7},{6,4},{7,5},{8,10},{9,11},{10,... | collective-permute-start | bytes 1572872 | tf_op jit(solution)/shard_map/ppermute | solution.py:266
  5.6 7.6 %collective-permute-start.2 = (bf16[128,256]{1,0:T(8,128)(2,1)}, bf16[128,256]{1,0:T(8,128)(2,1)S(1)}, u32[]{:S(2)}, u32[]{:S(2)}) collective-permute-start(bf16[128,256]{1,0:T(8,128)(2,1)} %get-tuple-element.44), channel_id=1, source_target_pairs={{0,4},{4,8},{8,12},{12,16},{16,20},{20,24},{24,28},{28,32},{32,36}... | collective-permute-start | bytes 196616 | tf_op jit(solution)/shard_map/ppermute | solution.py:314
  7.2 6.2 %copy-start.1 = (bf16[1024,256]{1,0:T(8,128)(2,1)S(1)}, bf16[1024,256]{1,0:T(8,128)(2,1)}, u32[]{:S(2)}) copy-start(bf16[1024,256]{1,0:T(8,128)(2,1)} %get-tuple-element.43.a0) | copy-start | bytes 1572868
  7.2 16.2 %copy-start.11 = (bf16[144,128]{1,0:T(8,128)(2,1)S(1)}, bf16[144,128]{1,0:T(8,128)(2,1)}, u32[]{:S(2)}) copy-start(bf16[144,128]{1,0:T(8,128)(2,1)} %constant.2.clone.spread_ref) | copy-start | bytes 110596
  8.2 0.8 copy-start.4
  13.2 7.0 %collective-permute-start.3 = (bf16[128,256]{1,0:T(8,128)(2,1)S(1)}, bf16[128,256]{1,0:T(8,128)(2,1)S(1)}, u32[]{:S(2)}, u32[]{:S(2)}) collective-permute-start(bf16[128,256]{1,0:T(8,128)(2,1)S(1)} %collective-permute-done.2.l0), channel_id=1, source_target_pairs={{0,2},{1,3},{2,0},{3,1},{4,6},{5,7},{6,4},{7,5},{8,10},{9,11},{10,... | collective-permute-start | bytes 196616 | tf_op jit(solution)/shard_map/ppermute | solution.py:266
  13.4 9.9 %collective-permute-start = (bf16[1024,256]{1,0:T(8,128)(2,1)S(1)}, bf16[1024,256]{1,0:T(8,128)(2,1)S(1)}, u32[]{:S(2)}, u32[]{:S(2)}) collective-permute-start(bf16[1024,256]{1,0:T(8,128)(2,1)S(1)} %copy-done.1), channel_id=1, source_target_pairs={{0,1},{1,0},{2,3},{3,2},{4,5},{5,4},{6,7},{7,6},{8,9},{9,8},{10,11... | collective-permute-start | bytes 1572872 | tf_op jit(solution)/shard_map/ppermute | solution.py:266
  20.2 3.3 %collective-permute-start.4 = (bf16[1024,256]{1,0:T(8,128)(2,1)S(1)}, bf16[1024,256]{1,0:T(8,128)(2,1)S(1)}, u32[]{:S(2)}, u32[]{:S(2)}) collective-permute-start(bf16[1024,256]{1,0:T(8,128)(2,1)S(1)} %collective-permute-done.1.a2), channel_id=1, source_target_pairs={{0,1},{1,0},{2,3},{3,2},{4,5},{5,4},{6,7},{7,6},{8,9},{9,8},{10,11... | collective-permute-start | bytes 1572872 | tf_op jit(solution)/shard_map/ppermute | solution.py:266
  21.7 1.6 %collective-permute-start.6 = (bf16[128,256]{1,0:T(8,128)(2,1)S(1)}, bf16[128,256]{1,0:T(8,128)(2,1)S(1)}, u32[]{:S(2)}, u32[]{:S(2)}) collective-permute-start(bf16[128,256]{1,0:T(8,128)(2,1)S(1)} %collective-permute-done.2.l0), channel_id=1, source_target_pairs={{0,1},{1,0},{2,3},{3,2},{4,5},{5,4},{6,7},{7,6},{8,9},{9,8},{10,11... | collective-permute-start | bytes 196616 | tf_op jit(solution)/shard_map/ppermute | solution.py:266
  21.7 1.7 %collective-permute-start.7 = (bf16[128,256]{1,0:T(8,128)(2,1)S(1)}, bf16[128,256]{1,0:T(8,128)(2,1)S(1)}, u32[]{:S(2)}, u32[]{:S(2)}) collective-permute-start(bf16[128,256]{1,0:T(8,128)(2,1)S(1)} %collective-permute-done.3.l2), channel_id=1, source_target_pairs={{0,1},{1,0},{2,3},{3,2},{4,5},{5,4},{6,7},{7,6},{8,9},{9,8},{10,11... | collective-permute-start | bytes 196616 | tf_op jit(solution)/shard_map/ppermute | solution.py:266
  27.7 0.8 copy-start.2
  28.5 24.7 %all-to-all-start = ((bf16[8,64,512]{2,1,0:T(8,128)(2,1)}), bf16[8,64,512]{2,1,0:T(8,128)(2,1)S(1)}, u32[]{:S(2)}, u32[]{:S(2)}) async-start(bf16[8,64,512]{2,1,0:T(8,128)(2,1)} %pool.1), calls=%async_computation | async-start | bytes 1048576 | tf_op jit(solution)/shard_map/all_to_all | solution.py:338
  35.3 20.5 %collective-permute-start.5 = (bf16[1536,256]{1,0:T(8,128)(2,1)}, bf16[1536,256]{1,0:T(8,128)(2,1)S(1)}, u32[]{:S(2)}, u32[]{:S(2)}) collective-permute-start(bf16[1536,256]{1,0:T(8,128)(2,1)} %get-tuple-element.51.b0), channel_id=1, source_target_pairs={{0,2},{1,3},{2,0},{3,1},{4,6},{5,7},{6,4},{7,5},{8,10},{9,11},{10,... | collective-permute-start | bytes 2359304 | tf_op jit(solution)/shard_map/ppermute | solution.py:266
  36.5 22.2 %collective-permute-start.8 = (bf16[1280,256]{1,0:T(8,128)(2,1)}, bf16[1280,256]{1,0:T(8,128)(2,1)S(1)}, u32[]{:S(2)}, u32[]{:S(2)}) collective-permute-start(bf16[1280,256]{1,0:T(8,128)(2,1)} %get-tuple-element.56), channel_id=1, source_target_pairs={{0,1},{1,0},{2,3},{3,2},{4,5},{5,4},{6,7},{7,6},{8,9},{9,8},{10,11... | collective-permute-start | bytes 1966088 | tf_op jit(solution)/shard_map/ppermute | solution.py:266
  53.3 2.5 %copy-start.3 = (bf16[1024,256]{1,0:T(8,128)(2,1)S(1)}, bf16[1024,256]{1,0:T(8,128)(2,1)}, u32[]{:S(2)}) copy-start(bf16[1024,256]{1,0:T(8,128)(2,1)} %copy-done.2) | copy-start | bytes 1572868
  53.3 10.5 %collective-permute-start.11 = (bf16[384,512]{1,0:T(8,128)(2,1)S(1)}, bf16[384,512]{1,0:T(8,128)(2,1)S(1)}, u32[]{:S(2)}, u32[]{:S(2)}) collective-permute-start(bf16[384,512]{1,0:T(8,128)(2,1)S(1)} %get-tuple-element.60), channel_id=1, source_target_pairs={{0,32},{4,36},{8,40},{12,44},{16,48},{20,52},{24,56},{28,60},{32,6... | collective-permute-start | bytes 1179656 | tf_op jit(solution)/shard_map/ppermute | solution.py:349
  55.8 13.5 %collective-permute-start.12 = (bf16[384,512]{1,0:T(8,128)(2,1)S(1)}, bf16[384,512]{1,0:T(8,128)(2,1)S(1)}, u32[]{:S(2)}, u32[]{:S(2)}) collective-permute-start(bf16[384,512]{1,0:T(8,128)(2,1)S(1)} %get-tuple-element.61), channel_id=1, source_target_pairs={{32,0},{36,4},{40,8},{44,12},{48,16},{52,20},{56,24},{60,28},{64,3... | collective-permute-start | bytes 1179656 | tf_op jit(solution)/shard_map/ppermute | solution.py:350
  55.8 1.0 copy-start.5
  56.9 3.1 %copy-start.7 = (bf16[1536,256]{1,0:T(8,128)(2,1)S(1)}, bf16[1536,256]{1,0:T(8,128)(2,1)}, u32[]{:S(2)}) copy-start(bf16[1536,256]{1,0:T(8,128)(2,1)} %get-tuple-element.51.b0) | copy-start | bytes 2359300
  57.6 2.0 %collective-permute-start.10 = (bf16[512,256]{1,0:T(8,128)(2,1)S(1)}, bf16[512,256]{1,0:T(8,128)(2,1)S(1)}, u32[]{:S(2)}, u32[]{:S(2)}) collective-permute-start(bf16[512,256]{1,0:T(8,128)(2,1)S(1)} %get-tuple-element.58), channel_id=1, source_target_pairs={{0,1},{1,0},{2,3},{3,2},{4,5},{5,4},{6,7},{7,6},{8,9},{9,8},{10,11... | collective-permute-start | bytes 786440 | tf_op jit(solution)/shard_map/ppermute | solution.py:266
  58.5 1.5 %collective-permute-start.9 = (bf16[512,256]{1,0:T(8,128)(2,1)S(1)}, bf16[512,256]{1,0:T(8,128)(2,1)S(1)}, u32[]{:S(2)}, u32[]{:S(2)}) collective-permute-start(bf16[512,256]{1,0:T(8,128)(2,1)S(1)} %get-tuple-element.57), channel_id=1, source_target_pairs={{0,1},{1,0},{2,3},{3,2},{4,5},{5,4},{6,7},{7,6},{8,9},{9,8},{10,11... | collective-permute-start | bytes 786440 | tf_op jit(solution)/shard_map/ppermute | solution.py:266
  71.5 7.4 %collective-permute-start.13 = (bf16[256,256]{1,0:T(8,128)(2,1)S(1)}, bf16[256,256]{1,0:T(8,128)(2,1)S(1)}, u32[]{:S(2)}, u32[]{:S(2)}) collective-permute-start(bf16[256,256]{1,0:T(8,128)(2,1)S(1)} %attend0.1.rest_0_.a0), channel_id=1, source_target_pairs={{0,2},{1,3},{2,0},{3,1},{4,6},{5,7},{6,4},{7,5},{8,10},{9,11},{10,... | collective-permute-start | bytes 393224 | tf_op jit(solution)/shard_map/ppermute | solution.py:266
  71.9 11.4 %collective-permute-start.18 = (bf16[512,256]{1,0:T(8,128)(2,1)S(1)}, bf16[512,256]{1,0:T(8,128)(2,1)S(1)}, u32[]{:S(2)}, u32[]{:S(2)}) collective-permute-start(bf16[512,256]{1,0:T(8,128)(2,1)S(1)} %get-tuple-element.67), channel_id=1, source_target_pairs={{0,1},{1,0},{2,3},{3,2},{4,5},{5,4},{6,7},{7,6},{8,9},{9,8},{10,11... | collective-permute-start | bytes 786440 | tf_op jit(solution)/shard_map/ppermute | solution.py:266
  77.4 8.0 %collective-permute-start.15 = (bf16[512,256]{1,0:T(8,128)(2,1)S(1)}, bf16[512,256]{1,0:T(8,128)(2,1)S(1)}, u32[]{:S(2)}, u32[]{:S(2)}) collective-permute-start(bf16[512,256]{1,0:T(8,128)(2,1)S(1)} %attend1.1.rest_0_.a0), channel_id=1, source_target_pairs={{0,2},{1,3},{2,0},{3,1},{4,6},{5,7},{6,4},{7,5},{8,10},{9,11},{10,... | collective-permute-start | bytes 786440 | tf_op jit(solution)/shard_map/ppermute | solution.py:266
  78.6 4.7 %collective-permute-start.16 = (bf16[256,256]{1,0:T(8,128)(2,1)S(1)}, bf16[256,256]{1,0:T(8,128)(2,1)S(1)}, u32[]{:S(2)}, u32[]{:S(2)}) collective-permute-start(bf16[256,256]{1,0:T(8,128)(2,1)S(1)} %attend0.1.rest_0_.a0), channel_id=1, source_target_pairs={{0,1},{1,0},{2,3},{3,2},{4,5},{5,4},{6,7},{7,6},{8,9},{9,8},{10,11... | collective-permute-start | bytes 393224 | tf_op jit(solution)/shard_map/ppermute | solution.py:266
  78.9 5.4 %copy-start = (bf16[2048,256]{1,0:T(8,128)(2,1)S(1)}, bf16[2048,256]{1,0:T(8,128)(2,1)}, u32[]{:S(2)}) copy-start(bf16[2048,256]{1,0:T(8,128)(2,1)} %tokens_ref.7) | copy-start | bytes 3145732
  78.9 5.4 %copy-start.6 = (bf16[256,256]{1,0:T(8,128)(2,1)S(1)}, bf16[256,256]{1,0:T(8,128)(2,1)}, u32[]{:S(2)}) copy-start(bf16[256,256]{1,0:T(8,128)(2,1)} %get-tuple-element.66.w0) | copy-start | bytes 393220
  82.4 11.0 %collective-permute-start.14 = (bf16[512,256]{1,0:T(8,128)(2,1)S(1)}, bf16[512,256]{1,0:T(8,128)(2,1)S(1)}, u32[]{:S(2)}, u32[]{:S(2)}) collective-permute-start(bf16[512,256]{1,0:T(8,128)(2,1)S(1)} %attend2.1.rest_0_.a0), channel_id=1, source_target_pairs={{0,2},{1,3},{2,0},{3,1},{4,6},{5,7},{6,4},{7,5},{8,10},{9,11},{10,... | collective-permute-start | bytes 786440 | tf_op jit(solution)/shard_map/ppermute | solution.py:266
  82.8 1.5 %collective-permute-start.17 = (bf16[256,256]{1,0:T(8,128)(2,1)S(1)}, bf16[256,256]{1,0:T(8,128)(2,1)S(1)}, u32[]{:S(2)}, u32[]{:S(2)}) collective-permute-start(bf16[256,256]{1,0:T(8,128)(2,1)S(1)} %collective-permute-done.13.rest_1_.a2), channel_id=1, source_target_pairs={{0,1},{1,0},{2,3},{3,2},{4,5},{5,4},{6,7},{7,6},{8,9},{9,8},{10,11... | collective-permute-start | bytes 393224 | tf_op jit(solution)/shard_map/ppermute | solution.py:266
  90.2 9.5 %collective-permute-start.20 = (bf16[768,256]{1,0:T(8,128)(2,1)S(1)}, bf16[768,256]{1,0:T(8,128)(2,1)S(1)}, u32[]{:S(2)}, u32[]{:S(2)}) collective-permute-start(bf16[768,256]{1,0:T(8,128)(2,1)S(1)} %attend3.1.a0), channel_id=1, source_target_pairs={{0,2},{1,3},{2,0},{3,1},{4,6},{5,7},{6,4},{7,5},{8,10},{9,11},{10,... | collective-permute-start | bytes 1179656 | tf_op jit(solution)/shard_map/ppermute | solution.py:266
  91.5 2.6 %collective-permute-start.23 = (bf16[512,256]{1,0:T(8,128)(2,1)S(1)}, bf16[512,256]{1,0:T(8,128)(2,1)S(1)}, u32[]{:S(2)}, u32[]{:S(2)}) collective-permute-start(bf16[512,256]{1,0:T(8,128)(2,1)S(1)} %attend1.1.rest_0_.a0), channel_id=1, source_target_pairs={{0,1},{1,0},{2,3},{3,2},{4,5},{5,4},{6,7},{7,6},{8,9},{9,8},{10,11... | collective-permute-start | bytes 786440 | tf_op jit(solution)/shard_map/ppermute | solution.py:266
  92.9 3.2 %collective-permute-start.21 = (bf16[512,256]{1,0:T(8,128)(2,1)S(1)}, bf16[512,256]{1,0:T(8,128)(2,1)S(1)}, u32[]{:S(2)}, u32[]{:S(2)}) collective-permute-start(bf16[512,256]{1,0:T(8,128)(2,1)S(1)} %attend2.1.rest_0_.a0), channel_id=1, source_target_pairs={{0,1},{1,0},{2,3},{3,2},{4,5},{5,4},{6,7},{7,6},{8,9},{9,8},{10,11... | collective-permute-start | bytes 786440 | tf_op jit(solution)/shard_map/ppermute | solution.py:266
  92.9 1.9 %collective-permute-start.24 = (bf16[512,256]{1,0:T(8,128)(2,1)S(1)}, bf16[512,256]{1,0:T(8,128)(2,1)S(1)}, u32[]{:S(2)}, u32[]{:S(2)}) collective-permute-start(bf16[512,256]{1,0:T(8,128)(2,1)S(1)} %collective-permute-done.15.rest_2_.a2), channel_id=1, source_target_pairs={{0,1},{1,0},{2,3},{3,2},{4,5},{5,4},{6,7},{7,6},{8,9},{9,8},{10,11... | collective-permute-start | bytes 786440 | tf_op jit(solution)/shard_map/ppermute | solution.py:266
  93.4 2.7 %collective-permute-start.22 = (bf16[512,256]{1,0:T(8,128)(2,1)S(1)}, bf16[512,256]{1,0:T(8,128)(2,1)S(1)}, u32[]{:S(2)}, u32[]{:S(2)}) collective-permute-start(bf16[512,256]{1,0:T(8,128)(2,1)S(1)} %collective-permute-done.14.a2), channel_id=1, source_target_pairs={{0,1},{1,0},{2,3},{3,2},{4,5},{5,4},{6,7},{7,6},{8,9},{9,8},{10,11... | collective-permute-start | bytes 786440 | tf_op jit(solution)/shard_map/ppermute | solution.py:266
  94.1 7.8 %collective-permute-start.19 = (bf16[768,256]{1,0:T(8,128)(2,1)S(1)}, bf16[768,256]{1,0:T(8,128)(2,1)S(1)}, u32[]{:S(2)}, u32[]{:S(2)}) collective-permute-start(bf16[768,256]{1,0:T(8,128)(2,1)S(1)} %attend3.1.a0), channel_id=1, source_target_pairs={{0,1},{1,0},{2,3},{3,2},{4,5},{5,4},{6,7},{7,6},{8,9},{9,8},{10,11... | collective-permute-start | bytes 1179656 | tf_op jit(solution)/shard_map/ppermute | solution.py:266
  99.7 3.4 %collective-permute-start.25 = (bf16[768,256]{1,0:T(8,128)(2,1)S(1)}, bf16[768,256]{1,0:T(8,128)(2,1)S(1)}, u32[]{:S(2)}, u32[]{:S(2)}) collective-permute-start(bf16[768,256]{1,0:T(8,128)(2,1)S(1)} %collective-permute-done.20.a2), channel_id=1, source_target_pairs={{0,1},{1,0},{2,3},{3,2},{4,5},{5,4},{6,7},{7,6},{8,9},{9,8},{10,11... | collective-permute-start | bytes 1179656 | tf_op jit(solution)/shard_map/ppermute | solution.py:266
